TPU v7x, 32 devices: a whole 2x2x4 slice. The times are simulated.
32 devices in a mesh: rep: 4 (over y, core), fsdp: 8 (over z, x).
Axes of the slice: x: 2, y: 2, z: 4, core: 2. Of those that a mesh axis runs over, the one named last changes fastest.
Arguments:
- tokens: bfloat16 [64, 1024, 1024], P(('rep', 'fsdp')), may hold values from -12 to 12
- lengths: int32 [64], P(('rep', 'fsdp')), may hold values from 384 to 1024, as said below
- cotangent: bfloat16 [64, 1024, 1024], P(('rep', 'fsdp')), may hold values from -6 to 6
- mix_weight: bfloat16 [1024, 3072], P('fsdp'), may hold values from -0.25 to 0.25
- mix_bias: bfloat16 [3072], P('fsdp'), may hold values from -1.75 to 1.75
- proj_weight: bfloat16 [1024, 1024], P('fsdp'), may hold values from -1.5 to 1.5
- proj_bias: bfloat16 [1024], P('fsdp'), may hold values from -1.75 to 1.75
- up_weight: bfloat16 [1024, 4096], P('fsdp'), may hold values from -0.1875 to 0.1875
- up_bias: bfloat16 [4096], P('fsdp'), may hold values from -1.75 to 1.75
- down_weight: bfloat16 [4096, 1024], P('fsdp'), may hold values from -0.09375 to 0.09375
- down_bias: bfloat16 [1024], P('fsdp'), may hold values from -1.75 to 1.75
- gain_attn: bfloat16 [1024], P('fsdp'), may hold values from 0.099609375 to 1.8984375
- shift_attn: bfloat16 [1024], P('fsdp'), may hold values from -1.75 to 1.75
- gain_mlp: bfloat16 [1024], P('fsdp'), may hold values from 0.099609375 to 1.8984375
- shift_mlp: bfloat16 [1024], P('fsdp'), may hold values from -1.75 to 1.75
Outputs:
- layer_out: bfloat16 [64, 1024, 1024], P(('rep', 'fsdp'))
- grad_tokens: float32 [64, 1024, 1024], P(('rep', 'fsdp'))
- grad_mix_weight: float32 [1024, 3072], P('fsdp')
- grad_mix_bias: float32 [3072], P('fsdp')
- grad_proj_weight: float32 [1024, 1024], P('fsdp')
- grad_proj_bias: float32 [1024], P('fsdp')
- grad_up_weight: float32 [1024, 4096], P('fsdp')
- grad_up_bias: float32 [4096], P('fsdp')
- grad_down_weight: float32 [4096, 1024], P('fsdp')
- grad_down_bias: float32 [1024], P('fsdp')
- grad_gain_attn: float32 [1024], P('fsdp')
- grad_shift_attn: float32 [1024], P('fsdp')
- grad_gain_mlp: float32 [1024], P('fsdp')
- grad_shift_mlp: float32 [1024], P('fsdp')
Inputs may be any that keep to these rules, and one draw needn't show every extreme that they name: `lengths`: the length of each micro-batch's sequence, a multiple of 128; its rows from the length on are padding; at least one micro-batch holds 1024 tokens.
All inputs are finite; a program needn't handle non-finite values.
Results may differ from a plain program's by a relative error of at most 0.017.
Values may be sent and summed in bfloat16 or wider, within the bound.
A program may use at most 512 MiB of HBM per device.

v0:
```python
import math

import jax
import jax.numpy as jnp
from jax import lax
from jax.sharding import PartitionSpec as P

HEADS = 16
HEAD = 64
ROT = 16


EPS = 1e-05
BASE = 10000.0


def as_sent(array):
    return jax.tree.map(lambda a: a.astype(jnp.bfloat16) if a.dtype == jnp.float32 else a, array)


def norm_rows(values, gain, shift):
    mean = jnp.mean(values, axis=-1, keepdims=True)
    centred = values - mean
    spread = jnp.mean(centred * centred, axis=-1, keepdims=True)
    return centred * lax.rsqrt(spread + EPS) * gain + shift


def angle_tables(rows, rotary):
    half = rotary // 2
    steps = jnp.arange(half, dtype=jnp.float32) * (2.0 / rotary)
    inverse = jnp.exp(-math.log(BASE) * steps)
    places = jnp.arange(rows, dtype=jnp.float32)
    angles = places[:, None] * inverse[None, :]
    return (jnp.cos(angles)[:, None, :], jnp.sin(angles)[:, None, :])


def rotate(values, cosines, sines):
    half = cosines.shape[-1]
    leading = values[..., :half]
    trailing = values[..., half : 2 * half]
    return jnp.concatenate(
        [
            leading * cosines - trailing * sines,
            trailing * cosines + leading * sines,
            values[..., 2 * half :],
        ],
        axis=-1,
    )


def causal_scores(query, keys):
    rows = query.shape[0]
    causal = lax.broadcasted_iota(jnp.int32, (rows, rows), 0) >= lax.broadcasted_iota(
        jnp.int32, (rows, rows), 1
    )
    scores = jnp.einsum("qhd,khd->hqk", query, keys, preferred_element_type=jnp.float32)
    return jnp.where(causal[None], scores, -1e30)


def forward(full, inputs, valid, cosines, sines):
    (
        mix_weight,
        mix_bias,
        proj_weight,
        proj_bias,
        up_weight,
        up_bias,
        down_weight,
        down_bias,
        gain_attn,
        shift_attn,
        gain_mlp,
        shift_mlp,
    ) = full
    rows, width = inputs.shape
    first = norm_rows(inputs, gain_attn.astype(jnp.float32), shift_attn.astype(jnp.float32)).astype(
        jnp.bfloat16
    )
    second = norm_rows(inputs, gain_mlp.astype(jnp.float32), shift_mlp.astype(jnp.float32)).astype(
        jnp.bfloat16
    )
    mixed = jnp.dot(first, mix_weight, preferred_element_type=jnp.float32) + mix_bias.astype(
        jnp.float32
    )
    mixed = mixed.reshape(rows, 3, HEADS, HEAD)
    query = (rotate(mixed[:, 0], cosines, sines) * HEAD ** (-0.5)).astype(jnp.bfloat16)
    keys = rotate(mixed[:, 1], cosines, sines).astype(jnp.bfloat16)
    values = mixed[:, 2].astype(jnp.bfloat16)
    scores = causal_scores(query, keys)
    peak = jnp.max(scores, axis=-1, keepdims=True)
    expo = jnp.exp(scores - peak)
    totals = jnp.sum(expo, axis=-1, keepdims=True)
    probs = expo / totals
    logsum = peak + jnp.log(totals)
    context = jnp.einsum(
        "hqk,khd->qhd", probs.astype(jnp.bfloat16), values, preferred_element_type=jnp.float32
    )
    context = context.astype(jnp.bfloat16).reshape(rows, width)
    attend = jnp.dot(context, proj_weight, preferred_element_type=jnp.float32) + proj_bias.astype(
        jnp.float32
    )
    hidden = jnp.dot(second, up_weight, preferred_element_type=jnp.float32) + up_bias.astype(
        jnp.float32
    )
    active = jax.nn.gelu(hidden, approximate=False).astype(jnp.bfloat16)
    feed = jnp.dot(active, down_weight, preferred_element_type=jnp.float32) + down_bias.astype(
        jnp.float32
    )
    result = valid[:, None] * (inputs + attend + feed)
    return (result, (first, second, query, keys, values, logsum, context, hidden, active))


def backward(full, kept, inputs, valid, upstream, cosines, sines):
    (
        mix_weight,
        mix_bias,
        proj_weight,
        proj_bias,
        up_weight,
        up_bias,
        down_weight,
        down_bias,
        gain_attn,
        shift_attn,
        gain_mlp,
        shift_mlp,
    ) = full
    first, second, query, keys, values, logsum, context, hidden, active = kept
    rows, width = inputs.shape
    outer = upstream * valid[:, None]
    outer_low = outer.astype(jnp.bfloat16)
    grad_proj_weight = jnp.einsum(
        "sd,se->de", context, outer_low, preferred_element_type=jnp.float32
    )
    grad_down_weight = jnp.einsum(
        "sf,se->fe", active, outer_low, preferred_element_type=jnp.float32
    )
    bias_grad = jnp.sum(outer, axis=0)
    grad_active = jnp.einsum(
        "se,fe->sf", outer_low, down_weight, preferred_element_type=jnp.float32
    )
    _, gelu_pull = jax.vjp(lambda value: jax.nn.gelu(value, approximate=False), hidden)
    grad_hidden = gelu_pull(grad_active)[0].astype(jnp.bfloat16)
    grad_up_weight = jnp.einsum(
        "sd,sf->df", second, grad_hidden, preferred_element_type=jnp.float32
    )
    grad_up_bias = jnp.sum(grad_hidden.astype(jnp.float32), axis=0)
    grad_second = jnp.einsum(
        "sf,df->sd", grad_hidden, up_weight, preferred_element_type=jnp.float32
    )
    grad_context = jnp.einsum(
        "se,de->sd", outer_low, proj_weight, preferred_element_type=jnp.float32
    )
    grad_context = grad_context.astype(jnp.bfloat16).reshape(rows, HEADS, HEAD)
    probs = jnp.exp(causal_scores(query, keys) - logsum)
    grad_probs = jnp.einsum(
        "qhd,khd->hqk", grad_context, values, preferred_element_type=jnp.float32
    )
    grad_scores = probs * (grad_probs - jnp.sum(probs * grad_probs, axis=-1, keepdims=True))
    grad_scores = grad_scores.astype(jnp.bfloat16)
    grad_values = jnp.einsum(
        "hqk,qhd->khd", probs.astype(jnp.bfloat16), grad_context, preferred_element_type=jnp.float32
    )
    grad_query = jnp.einsum("hqk,khd->qhd", grad_scores, keys, preferred_element_type=jnp.float32)
    grad_keys = jnp.einsum("hqk,qhd->khd", grad_scores, query, preferred_element_type=jnp.float32)
    blank = jnp.zeros_like(grad_query)
    _, query_pull = jax.vjp(lambda value: rotate(value, cosines, sines) * HEAD ** (-0.5), blank)
    _, keys_pull = jax.vjp(lambda value: rotate(value, cosines, sines), blank)
    grad_mixed = jnp.stack(
        [query_pull(grad_query)[0], keys_pull(grad_keys)[0], grad_values], axis=1
    )
    grad_mixed = grad_mixed.reshape(rows, 3 * width).astype(jnp.bfloat16)
    grad_mix_weight = jnp.einsum("sd,sc->dc", first, grad_mixed, preferred_element_type=jnp.float32)
    grad_mix_bias = jnp.sum(grad_mixed.astype(jnp.float32), axis=0)
    grad_first = jnp.einsum("sc,dc->sd", grad_mixed, mix_weight, preferred_element_type=jnp.float32)
    _, attn_pull = jax.vjp(
        norm_rows, inputs, gain_attn.astype(jnp.float32), shift_attn.astype(jnp.float32)
    )
    into_attn, grad_gain_attn, grad_shift_attn = attn_pull(grad_first)
    _, mlp_pull = jax.vjp(
        norm_rows, inputs, gain_mlp.astype(jnp.float32), shift_mlp.astype(jnp.float32)
    )
    into_mlp, grad_gain_mlp, grad_shift_mlp = mlp_pull(grad_second)
    grad_inputs = outer + into_attn + into_mlp
    grads = (
        grad_mix_weight,
        grad_mix_bias,
        grad_proj_weight,
        bias_grad,
        grad_up_weight,
        grad_up_bias,
        grad_down_weight,
        bias_grad,
        grad_gain_attn,
        grad_shift_attn,
        grad_gain_mlp,
        grad_shift_mlp,
    )
    return (grad_inputs, grads)


def body(
    tokens,
    lengths,
    cotangent,
    mix_weight,
    mix_bias,
    proj_weight,
    proj_bias,
    up_weight,
    up_bias,
    down_weight,
    down_bias,
    gain_attn,
    shift_attn,
    gain_mlp,
    shift_mlp,
):
    shards = (
        mix_weight,
        mix_bias,
        proj_weight,
        proj_bias,
        up_weight,
        up_bias,
        down_weight,
        down_bias,
        gain_attn,
        shift_attn,
        gain_mlp,
        shift_mlp,
    )
    rows = tokens.shape[1]
    groups = lax.axis_size("fsdp")
    cosines, sines = angle_tables(rows, ROT)
    places = jnp.arange(rows, dtype=jnp.int32)

    def micro(carry, batch):
        block, length, upstream = batch
        valid = (places < length).astype(jnp.float32)
        inputs = block.astype(jnp.float32)
        full = (
            lax.all_gather(shards[0], "fsdp", axis=0, tiled=True),
            lax.all_gather(shards[1], "fsdp", axis=0, tiled=True),
            lax.all_gather(shards[2], "fsdp", axis=0, tiled=True),
            lax.all_gather(shards[3], "fsdp", axis=0, tiled=True),
            lax.all_gather(shards[4], "fsdp", axis=0, tiled=True),
            lax.all_gather(shards[5], "fsdp", axis=0, tiled=True),
            lax.all_gather(shards[6], "fsdp", axis=0, tiled=True),
            lax.all_gather(shards[7], "fsdp", axis=0, tiled=True),
            lax.all_gather(shards[8], "fsdp", axis=0, tiled=True),
            lax.all_gather(shards[9], "fsdp", axis=0, tiled=True),
            lax.all_gather(shards[10], "fsdp", axis=0, tiled=True),
            lax.all_gather(shards[11], "fsdp", axis=0, tiled=True),
        )
        result, kept = forward(full, inputs, valid, cosines, sines)
        again = (
            lax.all_gather(shards[0], "fsdp", axis=0, tiled=True),
            lax.all_gather(shards[1], "fsdp", axis=0, tiled=True),
            lax.all_gather(shards[2], "fsdp", axis=0, tiled=True),
            lax.all_gather(shards[3], "fsdp", axis=0, tiled=True),
            lax.all_gather(shards[4], "fsdp", axis=0, tiled=True),
            lax.all_gather(shards[5], "fsdp", axis=0, tiled=True),
            lax.all_gather(shards[6], "fsdp", axis=0, tiled=True),
            lax.all_gather(shards[7], "fsdp", axis=0, tiled=True),
            lax.all_gather(shards[8], "fsdp", axis=0, tiled=True),
            lax.all_gather(shards[9], "fsdp", axis=0, tiled=True),
            lax.all_gather(shards[10], "fsdp", axis=0, tiled=True),
            lax.all_gather(shards[11], "fsdp", axis=0, tiled=True),
        )
        grad_inputs, grads = backward(
            again, kept, inputs, valid, upstream.astype(jnp.float32), cosines, sines
        )
        carry = tuple((total + extra for total, extra in zip(carry, grads)))
        return (carry, (result.astype(jnp.bfloat16), grad_inputs))

    start = tuple(
        (jnp.zeros((piece.shape[0] * groups,) + piece.shape[1:], jnp.float32) for piece in shards)
    )
    carry, (outputs, grad_tokens) = lax.scan(micro, start, (tokens, lengths, cotangent))
    carry = jax.tree.map(
        lambda part: part.astype(jnp.float32),
        lax.psum_scatter(as_sent(carry), "fsdp", scatter_dimension=0, tiled=True),
    )
    summed = jax.tree.map(lambda part: part.astype(jnp.float32), lax.psum(as_sent(carry), "rep"))
    return (
        outputs,
        grad_tokens,
        summed[0],
        summed[1],
        summed[2],
        summed[3],
        summed[4],
        summed[5],
        summed[6],
        summed[7],
        summed[8],
        summed[9],
        summed[10],
        summed[11],
    )


def solution(mesh):
    in_specs = (
        P(("rep", "fsdp"), None, None),
        P(("rep", "fsdp")),
        P(("rep", "fsdp"), None, None),
        P("fsdp", None),
        P("fsdp"),
        P("fsdp", None),
        P("fsdp"),
        P("fsdp", None),
        P("fsdp"),
        P("fsdp", None),
        P("fsdp"),
        P("fsdp"),
        P("fsdp"),
        P("fsdp"),
        P("fsdp"),
    )
    out_specs = (
        P(("rep", "fsdp"), None, None),
        P(("rep", "fsdp"), None, None),
        P("fsdp", None),
        P("fsdp"),
        P("fsdp", None),
        P("fsdp"),
        P("fsdp", None),
        P("fsdp"),
        P("fsdp", None),
        P("fsdp"),
        P("fsdp"),
        P("fsdp"),
        P("fsdp"),
        P("fsdp"),
    )
    return jax.shard_map(body, mesh=mesh, in_specs=in_specs, out_specs=out_specs, check_vma=False)
```

profile of v0, /device:TPU:0, one launch (start us, length us, event | category | flops | bytes accessed | tf_op | source)
XLA Modules:
  0.0 1899.2 jit_solution(2203115813240861611)
XLA Ops:
  8.2 1314.3 %while.40 = (s32[]{:T(128)}, f32[1024,3072]{1,0:T(8,128)}, f32[3072]{0:T(1024)}, f32[1024,1024]{1,0:T(8,128)}, f32[1024]{0:T(1024)S(1)}, /*index=5*/f32[1024,409...) while((s32[]{:T(128)}, f32[1024,3072]{1,0:T(8,128)}, ...), condition=%wide.region_17.18_spmd.clone.clone.clone.clone, body=%wide.region_0.17_spmd.clone.clone.clone.clone.sunk | while | flops 91074592768 | bytes 1485181568 | solution.py:280
  13.2 22.3 %all-gather.42 = bf16[8,1,128]{2,1,0:T(2,128)(2,1)S(1)} all-gather(bf16[1,1,128]{2,1,0:T(2,128)(2,1)S(1)} %bitcast.335), channel_id=1, replica_groups=mesh['rep'=4,'fsdp'=8] {'fsdp'}, dimensions={0}, use_global_device_ids=true | all-gather | bytes 2304 | tf_op jit(solution)/shard_map/while/body/eval_jaxpr/all_gather | solution.py:251
  35.6 16.3 all-gather.41
  51.9 18.4 all-gather.45
  70.8 16.4 all-gather.44
  87.8 18.2 all-gather.47
  106.6 16.6 all-gather.46
  129.2 26.5 %all-gather.40 = bf16[8,1,384]{2,1,0:T(2,128)(2,1)S(1)} all-gather(bf16[1,1,384]{2,1,0:T(2,128)(2,1)S(1)} %reshape.319), channel_id=1, replica_groups=mesh['rep'=4,'fsdp'=8] {'fsdp'}, dimensions={0}, use_global_device_ids=true | all-gather | bytes 6912 | tf_op jit(solution)/shard_map/while/body/eval_jaxpr/all_gather | solution.py:244
  155.7 26.4 %all-gather.43 = bf16[8,1,512]{2,1,0:T(2,128)(2,1)S(1)} all-gather(bf16[1,1,512]{2,1,0:T(2,128)(2,1)S(1)} %reshape.320), channel_id=1, replica_groups=mesh['rep'=4,'fsdp'=8] {'fsdp'}, dimensions={0}, use_global_device_ids=true | all-gather | bytes 9216 | tf_op jit(solution)/shard_map/while/body/eval_jaxpr/all_gather | solution.py:248
  189.1 13.1 broadcast_add_fusion.2
  202.2 12.7 copy.51
  222.4 24.5 %select_reduce_fusion.2 = (f32[16,1024]{1,0:T(8,128)S(1)}, f32[16,1024,1024]{1,2,0:T(8,128)}) fusion(pred[1024,1024]{0,1:T(8,128)(4,1)S(1)} %iota_compare_fusion.3, bf16[1024,16,48]{0,2,1:T(8,128)(2,1)S(1)} %slice.107, bf16[1024,16,8]{0,2,1:T(8,128)(2,1)S(1)} %get-tuple-element.934, bf16[1024,16,8]{0,2,1:T(8,128)(2,1)} %get-tuple-element.935, ...), kind=kOutput, calls=%fused_computation.9.clone.1 | convolution fusion | flops 2191507456 | bytes 74514432 | tf_op jit(solution)/shard_map/while/body/eval_jaxpr/qhd,khd->hqk/dot_general | solution.py:56
  246.9 21.9 %fusion.201 = f32[16,1024]{1,0:T(8,128)S(1)} fusion(f32[16,1024,1024]{1,2,0:T(8,128)} %get-tuple-element.938, f32[16,1024]{1,0:T(8,128)S(1)} %get-tuple-element.939, pred[1024,1024]{0,1:T(8,128)(4,1)S(1)} %iota_compare_fusion.3), kind=kLoop, calls=%fused_computation.8.clone.1 | loop fusion | flops 50315264 | bytes 68288512 | tf_op jit(solution)/shard_map/while/body/eval_jaxpr/reduce_sum | solution.py:92
  268.9 26.9 %fusion.203 = bf16[16,64,1024]{2,1,0:T(8,128)(2,1)} fusion(f32[16,1024,1024]{1,2,0:T(8,128)} %get-tuple-element.938, f32[16,1024]{1,0:T(8,128)S(1)} %fusion.201, f32[16,1024]{1,0:T(8,128)S(1)} %get-tuple-element.939, pred[1024,1024]{0,1:T(8,128)(4,1)S(1)} %iota_compare_fusion.3, f32[1024,3,16,64]{0,3,2,1:T(8,128)} %bitcast.310), kind=kOutput, calls=%fused_computation.111.clone.1 | convolution fusion | flops 2215641088 | bytes 72482816 | tf_op jit(solution)/shard_map/while/body/eval_jaxpr/hqk,khd->qhd/dot_general | solution.py:95
  295.7 26.9 %fusion.202 = bf16[1024,1,16,64]{0,3,2,1:T(8,128)(2,1)} fusion(bf16[1024,16,64]{0,2,1:T(8,128)(2,1)S(1)} %bitcast.314, f32[16,1024,1024]{1,2,0:T(8,128)} %get-tuple-element.938, f32[16,1024]{1,0:T(8,128)S(1)} %log_add_fusion.2, pred[1024,1024]{0,1:T(8,128)(4,1)S(1)} %iota_compare_fusion.3), kind=kOutput, calls=%fused_computation.92.clone.1 | convolution fusion | flops 2197815296 | bytes 72417280 | tf_op jit(solution)/shard_map/while/body/eval_jaxpr/hqk,qhd->khd/dot_general | solution.py:161
  322.6 48.6 %multiply_reduce_fusion.2 = (f32[16,1024]{1,0:T(8,128)S(1)}, f32[16,1024,1024]{1,2,0:T(8,128)}) fusion(f32[16,1024,1024]{1,2,0:T(8,128)} %get-tuple-element.938, f32[16,1024]{1,0:T(8,128)S(1)} %log_add_fusion.2, pred[1024,1024]{0,1:T(8,128)(4,1)S(1)} %iota_compare_fusion.3, bf16[1024,16,64]{0,2,1:T(8,128)(2,1)S(1)} %bitcast.315, ...), kind=kOutput, calls=%fused_computation.5.clone.2 | convolution fusion | flops 2214576128 | bytes 139591680 | tf_op jit(solution)/shard_map/while/body/eval_jaxpr/qhd,khd->hqk/dot_general | solution.py:156
  371.2 54.2 %multiply_convert_fusion.4 = bf16[16,1024,1024]{1,2,0:T(8,128)(2,1)} fusion(f32[16,1024,1024]{1,2,0:T(8,128)} %get-tuple-element.940, f32[16,1024,1024]{1,2,0:T(8,128)} %get-tuple-element.938, f32[16,1024]{1,0:T(8,128)S(1)} %get-tuple-element.941, f32[16,1024]{1,0:T(8,128)S(1)} %log_add_fusion.2, pred[1024,1024]{0,1:T(8,128)(4,1)S(1)} %iota_compare_fusion.3), kind=kLoop, calls=%fused_computation.4.clone.1 | loop fusion | flops 83886080 | bytes 168951808 | tf_op jit(solution)/shard_map/while/body/eval_jaxpr/convert_element_type | solution.py:160
  425.4 19.9 %convolution_bitcast_fusion.2 = f32[1024,16,64]{0,2,1:T(8,128)} fusion(bf16[16,1024,1024]{1,2,0:T(8,128)(2,1)} %multiply_convert_fusion.4, f32[1024,16,48]{0,2,1:T(8,128)} %copy-done, f32[1024,16,8]{0,2,1:T(8,128)S(1)} %copy-done.10, f32[1024,16,8]{0,2,1:T(8,128)S(1)} %copy-done.8), kind=kOutput, calls=%fused_computation.93.clone.1 | convolution fusion | flops 2151677952 | bytes 41943040 | tf_op jit(solution)/shard_map/while/body/eval_jaxpr/hqk,qhd->khd/dot_general | solution.py:165
  445.4 18.5 multiply_bitcast_fusion.2
  485.8 13.1 select_add_fusion.23
  499.0 51.1 %multiply_convert_fusion.5 = (bf16[1024,4096]{1,0:T(8,128)(2,1)}, f32[1024,4096]{1,0:T(8,128)}, f32[1024,4096]{1,0:T(8,128)}) fusion(f32[4096]{0:T(1024)S(1)} %bitcast.328, bf16[1024,4096]{1,0:T(8,128)(2,1)} %all-gather.57.cloned.1.call-done, f32[1024]{0:T(1024)S(1)} %bitcast.321, f32[1024]{0:T(1024)S(1)} %bitcast.316, f32[1024]{0:T(1024)S(1)} %copy-done.21, ...), kind=kOutput, calls=%fused_computation.18.clone.1 | convolution fusion | flops 8873050112 | bytes 52461572 | tf_op jit(solution)/shard_map/while/body/eval_jaxpr/dot_general | solution.py:102
  550.1 24.2 %convert_reduce_fusion.8 = (f32[4096]{0:T(1024)S(1)}, bf16[1024,4096]{1,0:T(8,128)(2,1)}) fusion(f32[1024,4096]{1,0:T(8,128)} %get-tuple-element.950, bf16[4096,1024]{1,0:T(8,128)(2,1)} %all-gather.59.cloned.1.call-done, f32[1024]{0:T(1024)S(1)} %copy-done.37, bf16[2,1024,1024]{2,1,0:T(8,128)(2,1)} %get-tuple-element.1053, s32[]{:T(128)S(6)} %copy.69, ...), kind=kOutput, calls=%fused_computation.19.clone.1 | convolution fusion | flops 8664379392 | bytes 52465668 | tf_op jit(solution)/shard_map/while/body/eval_jaxpr/se,fe->sf/dot_general | solution.py:139
  574.3 16.6 select_add_fusion.27
  590.9 13.3 fusion.204
  604.2 13.6 fusion.205
  622.2 16.7 select_add_fusion.29
  639.0 6.8 fusion.209
  647.1 14.0 fusion.208
  667.7 16.3 all-gather.42
  684.0 18.3 all-gather.41
  702.3 16.3 all-gather.45
  719.2 18.4 all-gather.44
  738.3 16.3 all-gather.47
  755.2 18.3 all-gather.46
  779.4 26.5 %all-gather.40 = bf16[8,1,384]{2,1,0:T(2,128)(2,1)S(1)} all-gather(bf16[1,1,384]{2,1,0:T(2,128)(2,1)S(1)} %reshape.319), channel_id=1, replica_groups=mesh['rep'=4,'fsdp'=8] {'fsdp'}, dimensions={0}, use_global_device_ids=true | all-gather | bytes 6912 | tf_op jit(solution)/shard_map/while/body/eval_jaxpr/all_gather | solution.py:244
  805.9 26.6 %all-gather.43 = bf16[8,1,512]{2,1,0:T(2,128)(2,1)S(1)} all-gather(bf16[1,1,512]{2,1,0:T(2,128)(2,1)S(1)} %reshape.320), channel_id=1, replica_groups=mesh['rep'=4,'fsdp'=8] {'fsdp'}, dimensions={0}, use_global_device_ids=true | all-gather | bytes 9216 | tf_op jit(solution)/shard_map/while/body/eval_jaxpr/all_gather | solution.py:248
  839.5 13.1 broadcast_add_fusion.2
  852.6 12.8 copy.51
  872.0 24.5 %select_reduce_fusion.2 = (f32[16,1024]{1,0:T(8,128)S(1)}, f32[16,1024,1024]{1,2,0:T(8,128)}) fusion(pred[1024,1024]{0,1:T(8,128)(4,1)S(1)} %iota_compare_fusion.3, bf16[1024,16,48]{0,2,1:T(8,128)(2,1)S(1)} %slice.107, bf16[1024,16,8]{0,2,1:T(8,128)(2,1)S(1)} %get-tuple-element.934, bf16[1024,16,8]{0,2,1:T(8,128)(2,1)} %get-tuple-element.935, ...), kind=kOutput, calls=%fused_computation.9.clone.1 | convolution fusion | flops 2191507456 | bytes 74514432 | tf_op jit(solution)/shard_map/while/body/eval_jaxpr/qhd,khd->hqk/dot_general | solution.py:56
  896.5 21.9 %fusion.201 = f32[16,1024]{1,0:T(8,128)S(1)} fusion(f32[16,1024,1024]{1,2,0:T(8,128)} %get-tuple-element.938, f32[16,1024]{1,0:T(8,128)S(1)} %get-tuple-element.939, pred[1024,1024]{0,1:T(8,128)(4,1)S(1)} %iota_compare_fusion.3), kind=kLoop, calls=%fused_computation.8.clone.1 | loop fusion | flops 50315264 | bytes 68288512 | tf_op jit(solution)/shard_map/while/body/eval_jaxpr/reduce_sum | solution.py:92
  918.5 27.1 %fusion.203 = bf16[16,64,1024]{2,1,0:T(8,128)(2,1)} fusion(f32[16,1024,1024]{1,2,0:T(8,128)} %get-tuple-element.938, f32[16,1024]{1,0:T(8,128)S(1)} %fusion.201, f32[16,1024]{1,0:T(8,128)S(1)} %get-tuple-element.939, pred[1024,1024]{0,1:T(8,128)(4,1)S(1)} %iota_compare_fusion.3, f32[1024,3,16,64]{0,3,2,1:T(8,128)} %bitcast.310), kind=kOutput, calls=%fused_computation.111.clone.1 | convolution fusion | flops 2215641088 | bytes 72482816 | tf_op jit(solution)/shard_map/while/body/eval_jaxpr/hqk,khd->qhd/dot_general | solution.py:95
  945.6 26.5 %fusion.202 = bf16[1024,1,16,64]{0,3,2,1:T(8,128)(2,1)} fusion(bf16[1024,16,64]{0,2,1:T(8,128)(2,1)S(1)} %bitcast.314, f32[16,1024,1024]{1,2,0:T(8,128)} %get-tuple-element.938, f32[16,1024]{1,0:T(8,128)S(1)} %log_add_fusion.2, pred[1024,1024]{0,1:T(8,128)(4,1)S(1)} %iota_compare_fusion.3), kind=kOutput, calls=%fused_computation.92.clone.1 | convolution fusion | flops 2197815296 | bytes 72417280 | tf_op jit(solution)/shard_map/while/body/eval_jaxpr/hqk,qhd->khd/dot_general | solution.py:161
  972.1 48.7 %multiply_reduce_fusion.2 = (f32[16,1024]{1,0:T(8,128)S(1)}, f32[16,1024,1024]{1,2,0:T(8,128)}) fusion(f32[16,1024,1024]{1,2,0:T(8,128)} %get-tuple-element.938, f32[16,1024]{1,0:T(8,128)S(1)} %log_add_fusion.2, pred[1024,1024]{0,1:T(8,128)(4,1)S(1)} %iota_compare_fusion.3, bf16[1024,16,64]{0,2,1:T(8,128)(2,1)S(1)} %bitcast.315, ...), kind=kOutput, calls=%fused_computation.5.clone.2 | convolution fusion | flops 2214576128 | bytes 139591680 | tf_op jit(solution)/shard_map/while/body/eval_jaxpr/qhd,khd->hqk/dot_general | solution.py:156
  1020.8 54.4 %multiply_convert_fusion.4 = bf16[16,1024,1024]{1,2,0:T(8,128)(2,1)} fusion(f32[16,1024,1024]{1,2,0:T(8,128)} %get-tuple-element.940, f32[16,1024,1024]{1,2,0:T(8,128)} %get-tuple-element.938, f32[16,1024]{1,0:T(8,128)S(1)} %get-tuple-element.941, f32[16,1024]{1,0:T(8,128)S(1)} %log_add_fusion.2, pred[1024,1024]{0,1:T(8,128)(4,1)S(1)} %iota_compare_fusion.3), kind=kLoop, calls=%fused_computation.4.clone.1 | loop fusion | flops 83886080 | bytes 168951808 | tf_op jit(solution)/shard_map/while/body/eval_jaxpr/convert_element_type | solution.py:160
  1075.2 19.7 %convolution_bitcast_fusion.2 = f32[1024,16,64]{0,2,1:T(8,128)} fusion(bf16[16,1024,1024]{1,2,0:T(8,128)(2,1)} %multiply_convert_fusion.4, f32[1024,16,48]{0,2,1:T(8,128)} %copy-done, f32[1024,16,8]{0,2,1:T(8,128)S(1)} %copy-done.10, f32[1024,16,8]{0,2,1:T(8,128)S(1)} %copy-done.8), kind=kOutput, calls=%fused_computation.93.clone.1 | convolution fusion | flops 2151677952 | bytes 41943040 | tf_op jit(solution)/shard_map/while/body/eval_jaxpr/hqk,qhd->khd/dot_general | solution.py:165
  1094.9 18.5 multiply_bitcast_fusion.2
  1135.5 14.9 select_add_fusion.23
  1150.5 51.2 %multiply_convert_fusion.5 = (bf16[1024,4096]{1,0:T(8,128)(2,1)}, f32[1024,4096]{1,0:T(8,128)}, f32[1024,4096]{1,0:T(8,128)}) fusion(f32[4096]{0:T(1024)S(1)} %bitcast.328, bf16[1024,4096]{1,0:T(8,128)(2,1)} %all-gather.57.cloned.1.call-done, f32[1024]{0:T(1024)S(1)} %bitcast.321, f32[1024]{0:T(1024)S(1)} %bitcast.316, f32[1024]{0:T(1024)S(1)} %copy-done.21, ...), kind=kOutput, calls=%fused_computation.18.clone.1 | convolution fusion | flops 8873050112 | bytes 52461572 | tf_op jit(solution)/shard_map/while/body/eval_jaxpr/dot_general | solution.py:102
  1201.6 24.1 %convert_reduce_fusion.8 = (f32[4096]{0:T(1024)S(1)}, bf16[1024,4096]{1,0:T(8,128)(2,1)}) fusion(f32[1024,4096]{1,0:T(8,128)} %get-tuple-element.950, bf16[4096,1024]{1,0:T(8,128)(2,1)} %all-gather.59.cloned.1.call-done, f32[1024]{0:T(1024)S(1)} %copy-done.37, bf16[2,1024,1024]{2,1,0:T(8,128)(2,1)} %get-tuple-element.1053, s32[]{:T(128)S(6)} %copy.69, ...), kind=kOutput, calls=%fused_computation.19.clone.1 | convolution fusion | flops 8664379392 | bytes 52465668 | tf_op jit(solution)/shard_map/while/body/eval_jaxpr/se,fe->sf/dot_general | solution.py:139
  1225.8 19.0 %select_add_fusion.27 = f32[1024,4096]{1,0:T(8,128)} fusion(f32[1024,4096]{1,0:T(8,128)} %get-tuple-element.1005, pred[]{:T(512)S(6)} %compare.11, bf16[1024,4096]{1,0:T(8,128)(2,1)} %get-tuple-element.952, f32[1024]{0:T(1024)S(1)} %bitcast.322, f32[1024]{0:T(1024)S(1)} %bitcast.317, f32[1024]{0:T(1024)S(1)} %copy-done.21, f32[1024]{0:T(1024)S(1)} %copy-done.18, ...), kind=kOutput, calls=%fused_computation.17.clone.1 | convolution fusion | flops 8604614656 | bytes 44056580 | tf_op jit(solution)/shard_map/while/body/eval_jaxpr/sd,sf->df/dot_general | solution.py:144
  1244.8 13.1 fusion.204
  1257.9 13.6 fusion.205
  1275.8 19.1 %select_add_fusion.29 = f32[4096,1024]{1,0:T(8,128)} fusion(f32[4096,1024]{1,0:T(8,128)} %get-tuple-element.1007, pred[]{:T(512)S(6)} %compare.11, bf16[1024,4096]{1,0:T(8,128)(2,1)} %get-tuple-element.954, f32[1024]{0:T(1024)S(1)} %copy-done.37, bf16[2,1024,1024]{2,1,0:T(8,128)(2,1)} %get-tuple-element.1053, s32[]{:T(128)S(6)} %copy.69), kind=kOutput, calls=%fused_computation.16.clone.1 | convolution fusion | flops 8601468928 | bytes 44044292 | tf_op jit(solution)/shard_map/while/body/eval_jaxpr/sf,se->fe/dot_general | solution.py:135
  1295.1 6.8 fusion.209
  1303.2 14.0 fusion.208
  1326.5 8.2 convert_element_type.220
  1334.8 9.1 convert_element_type.228
  1343.9 9.2 convert_element_type.232
  1353.3 38.7 %reduce-scatter.7.cloned.1.call-done = bf16[128,1024]{1,0:T(8,128)(2,1)} async-done(((bf16[1024,1024]{1,0:T(8,128)(2,1)}), bf16[128,1024]{1,0:T(8,128)(2,1)}) %reduce-scatter.7.cloned.1.call-update) | async-done | bytes 262160 | tf_op jit(solution)/shard_map/reduce_scatter | solution.py:283
  1392.0 120.1 %reduce-scatter.5.cloned.1.call-done = bf16[128,3072]{1,0:T(8,128)(2,1)} async-done(((bf16[1024,3072]{1,0:T(8,128)(2,1)}), bf16[128,3072]{1,0:T(8,128)(2,1)}) %reduce-scatter.5.cloned.1.call-update) | async-done | bytes 786448 | tf_op jit(solution)/shard_map/reduce_scatter | solution.py:283
  1512.1 149.8 %reduce-scatter.9.cloned.1.call-done = bf16[128,4096]{1,0:T(8,128)(2,1)} async-done(((bf16[1024,4096]{1,0:T(8,128)(2,1)}), bf16[128,4096]{1,0:T(8,128)(2,1)}) %reduce-scatter.9.cloned.1.call-update) | async-done | bytes 1048592 | tf_op jit(solution)/shard_map/reduce_scatter | solution.py:283
  1661.9 150.2 %reduce-scatter.11.cloned.1.call-done = bf16[512,1024]{1,0:T(8,128)(2,1)} async-done(((bf16[4096,1024]{1,0:T(8,128)(2,1)}), bf16[512,1024]{1,0:T(8,128)(2,1)}) %reduce-scatter.11.cloned.1.call-update) | async-done | bytes 1048592 | tf_op jit(solution)/shard_map/reduce_scatter | solution.py:283
  1814.8 35.2 %all-reduce.14 = (bf16[3072]{0:T(1024)(128)(2,1)S(1)}, bf16[1024]{0:T(1024)(128)(2,1)S(1)}, bf16[4096]{0:T(1024)(128)(2,1)S(1)}, bf16[1024]{0:T(1024)(128)(2,1)S...) all-reduce(bf16[3072]{0:T(1024)(128)(2,1)S(1)} %convert_element_typ, ...), channel_id=3, replica_groups=mesh['rep'=4,'fsdp'=8] {'fsdp'}, use_global_device_ids=true, to_apply=%region_20.21.clone | all-reduce | flops 13312 | bytes 53248
  1860.6 22.0 %all-reduce.19.cloned.1.call-done = (bf16[128,3072]{1,0:T(8,128)(2,1)}, bf16[128,1024]{1,0:T(8,128)(2,1)}, bf16[128,4096]{1,0:T(8,128)(2,1)}, bf16[512,1024]{1,0:T(8,128)(2,1)}) async-done(((bf16[128,3072]{1,0:T(8,128)(2,1)}, bf16[128,1024]{1,0:T(8,128)(2,1)}, bf16[128,4096]{1,0:T(8,128)(2,1)}, bf16[512,1024]{1,0:T(8,128)(2,1)}), (bf16[128,3072]{1,0:T(8,128)(2,1)}, bf16[128,1024]{1,0:T(8,128)(2,1)}, ...) | async-done | bytes 3145744 | tf_op jit(solution)/shard_map/psum | solution.py:285
  (484 shorter events, 134.7 us)
Async XLA Ops:
  8.7 174.0 %copy-start.67 = (f32[8]{0:T(128)}, f32[8]{0:T(128)S(1)}, u32[]{:S(2)}) copy-start(f32[8]{0:T(128)S(1)} %get-tuple-element.1063) | copy-start | bytes 100 | tf_op jit(solution)/shard_map/while
  8.7 26.8 %copy-start.70 = (bf16[128]{0:T(256)(128)(2,1)S(1)}, bf16[128]{0:T(256)(128)(2,1)}, u32[]{:S(2)}) copy-start(bf16[128]{0:T(256)(128)(2,1)} %get-tuple-element.1050) | copy-start | bytes 772 | tf_op jit(solution)/shard_map/while
  8.8 43.1 %copy-start.71 = (bf16[128]{0:T(256)(128)(2,1)S(1)}, bf16[128]{0:T(256)(128)(2,1)}, u32[]{:S(2)}) copy-start(bf16[128]{0:T(256)(128)(2,1)} %get-tuple-element.1056) | copy-start | bytes 772 | tf_op jit(solution)/shard_map/while
  8.8 62.1 %copy-start.72 = (bf16[128]{0:T(256)(128)(2,1)S(1)}, bf16[128]{0:T(256)(128)(2,1)}, u32[]{:S(2)}) copy-start(bf16[128]{0:T(256)(128)(2,1)} %get-tuple-element.1057) | copy-start | bytes 772 | tf_op jit(solution)/shard_map/while
  8.8 79.0 %copy-start.73 = (bf16[128]{0:T(256)(128)(2,1)S(1)}, bf16[128]{0:T(256)(128)(2,1)}, u32[]{:S(2)}) copy-start(bf16[128]{0:T(256)(128)(2,1)} %get-tuple-element.1061) | copy-start | bytes 772 | tf_op jit(solution)/shard_map/while
  8.8 97.9 %copy-start.74 = (bf16[128]{0:T(256)(128)(2,1)S(1)}, bf16[128]{0:T(256)(128)(2,1)}, u32[]{:S(2)}) copy-start(bf16[128]{0:T(256)(128)(2,1)} %get-tuple-element.1062) | copy-start | bytes 772 | tf_op jit(solution)/shard_map/while
  8.8 174.2 %all-gather.53.cloned.1.call-start = ((), (), s32[]{:S(2)}) async-start(), calls=%async_computation.9 | async-start | bytes 2359296 | tf_op jit(solution)/shard_map/while/body/eval_jaxpr/all_gather | solution.py:260
  9.5 179.5 %all-gather.55.cloned.1.call-start = ((), (), s32[]{:S(2)}) async-start(), calls=%async_computation.10 | async-start | bytes 7077888 | tf_op jit(solution)/shard_map/while/body/eval_jaxpr/all_gather | solution.py:243
  10.3 488.6 %all-gather.57.cloned.1.call-start = ((), (), s32[]{:S(2)}) async-start(), calls=%async_computation.11 | async-start | bytes 9437184 | tf_op jit(solution)/shard_map/while/body/eval_jaxpr/all_gather | solution.py:247
  11.0 539.1 %all-gather.59.cloned.1.call-start = ((), (), s32[]{:S(2)}) async-start(), calls=%async_computation.12 | async-start | bytes 9437184 | tf_op jit(solution)/shard_map/while/body/eval_jaxpr/all_gather | solution.py:264
  13.2 175.8 %copy-start.35 = (f32[1024]{0:T(1024)}, f32[1024]{0:T(1024)S(1)}, u32[]{:S(2)}) copy-start(f32[1024]{0:T(1024)S(1)} %fusion.198) | copy-start | bytes 12292 | tf_op jit(solution)/shard_map/while
  35.6 153.5 %copy-start.32 = (f32[8,1,128]{2,1,0:T(1,128)}, f32[8,1,128]{2,1,0:T(1,128)S(1)}, u32[]{:S(2)}) copy-start(f32[8,1,128]{2,1,0:T(1,128)S(1)} %convert_element_type.636) | copy-start | bytes 12292 | tf_op jit(solution)/shard_map/while
  51.9 137.2 %copy-start.63 = (f32[8,1,128]{2,1,0:T(1,128)}, f32[8,1,128]{2,1,0:T(1,128)S(1)}, u32[]{:S(2)}) copy-start(f32[8,1,128]{2,1,0:T(1,128)S(1)} %convert_element_type.635) | copy-start | bytes 12292 | tf_op jit(solution)/shard_map/while
  125.8 63.3 %copy-start.17 = (f32[1024]{0:T(1024)}, f32[1024]{0:T(1024)S(1)}, u32[]{:S(2)}) copy-start(f32[1024]{0:T(1024)S(1)} %broadcast_multiply_fusion.2) | copy-start | bytes 12292 | tf_op jit(solution)/shard_map/while
  129.2 53.5 %copy-start.30 = (f32[1024]{0:T(1024)}, f32[1024]{0:T(1024)S(1)}, u32[]{:S(2)}) copy-start(f32[1024]{0:T(1024)S(1)} %get-tuple-element.929) | copy-start | bytes 12292 | tf_op jit(solution)/shard_map/while
  129.2 59.9 %copy-start.20 = (f32[1024]{0:T(1024)}, f32[1024]{0:T(1024)S(1)}, u32[]{:S(2)}) copy-start(f32[1024]{0:T(1024)S(1)} %fusion.200) | copy-start | bytes 12292 | tf_op jit(solution)/shard_map/while
  182.9 38.0 %copy-start.23 = (f32[1024,8]{0,1:T(8,128)}, f32[1024,8]{0,1:T(8,128)S(1)}, u32[]{:S(2)}) copy-start(f32[1024,8]{0,1:T(8,128)S(1)} %get-tuple-element.933) | copy-start | bytes 98308 | tf_op jit(solution)/shard_map/while
  182.9 38.0 %copy-start.25 = (f32[1024,8]{0,1:T(8,128)}, f32[1024,8]{0,1:T(8,128)S(1)}, u32[]{:S(2)}) copy-start(f32[1024,8]{0,1:T(8,128)S(1)} %get-tuple-element.932) | copy-start | bytes 98308 | tf_op jit(solution)/shard_map/while
  220.9 26.0 %copy-start = (f32[1024,16,48]{0,2,1:T(8,128)}, f32[1024,16,48]{0,2,1:T(8,128)S(1)}, u32[]{:S(2)}) copy-start(f32[1024,16,48]{0,2,1:T(8,128)S(1)} %slice.108) | copy-start | bytes 9437188 | tf_op jit(solution)/shard_map/while
  222.4 24.5 %copy-start.7 = (f32[1024,16,8]{0,2,1:T(8,128)}, f32[1024,16,8]{0,2,1:T(8,128)S(1)}, u32[]{:S(2)}) copy-start(f32[1024,16,8]{0,2,1:T(8,128)S(1)} %get-tuple-element.937) | copy-start | bytes 1572868 | tf_op jit(solution)/shard_map/while
  222.4 24.5 %copy-start.9 = (f32[1024,16,8]{0,2,1:T(8,128)}, f32[1024,16,8]{0,2,1:T(8,128)S(1)}, u32[]{:S(2)}) copy-start(f32[1024,16,8]{0,2,1:T(8,128)S(1)} %get-tuple-element.936) | copy-start | bytes 1572868 | tf_op jit(solution)/shard_map/while
  222.4 24.6 %copy-start.13 = (bf16[1024,16,8]{0,2,1:T(8,128)(2,1)}, bf16[1024,16,8]{0,2,1:T(8,128)(2,1)S(1)}, u32[]{:S(2)}) copy-start(bf16[1024,16,8]{0,2,1:T(8,128)(2,1)S(1)} %get-tuple-element.934) | copy-start | bytes 786436 | tf_op jit(solution)/shard_map/while
  268.8 26.9 %copy-start.12 = (bf16[1024,1024]{0,1:T(8,128)(2,1)S(1)}, bf16[1024,1024]{0,1:T(8,128)(2,1)}, u32[]{:S(2)}) copy-start(bf16[1024,1024]{0,1:T(8,128)(2,1)} %convolution_convert_fusion.2) | copy-start | bytes 6291460 | tf_op jit(solution)/shard_map/while
  371.2 54.2 %copy-start.8 = (f32[1024,16,8]{0,2,1:T(8,128)S(1)}, f32[1024,16,8]{0,2,1:T(8,128)}, u32[]{:S(2)}) copy-start(f32[1024,16,8]{0,2,1:T(8,128)} %copy-done.7) | copy-start | bytes 1572868 | tf_op jit(solution)/shard_map/while
  371.2 54.2 %copy-start.10 = (f32[1024,16,8]{0,2,1:T(8,128)S(1)}, f32[1024,16,8]{0,2,1:T(8,128)}, u32[]{:S(2)}) copy-start(f32[1024,16,8]{0,2,1:T(8,128)} %copy-done.9) | copy-start | bytes 1572868 | tf_op jit(solution)/shard_map/while
  498.9 51.2 %copy-start.37 = (f32[1024]{0:T(1024)S(1)}, f32[1024]{0:T(1024)}, u32[]{:S(2)}) copy-start(f32[1024]{0:T(1024)} %copy-done.35) | copy-start | bytes 12292 | tf_op jit(solution)/shard_map/while
  663.3 169.8 %copy-start.67 = (f32[8]{0:T(128)}, f32[8]{0:T(128)S(1)}, u32[]{:S(2)}) copy-start(f32[8]{0:T(128)S(1)} %get-tuple-element.1063) | copy-start | bytes 100 | tf_op jit(solution)/shard_map/while
  663.4 20.7 %copy-start.70 = (bf16[128]{0:T(256)(128)(2,1)S(1)}, bf16[128]{0:T(256)(128)(2,1)}, u32[]{:S(2)}) copy-start(bf16[128]{0:T(256)(128)(2,1)} %get-tuple-element.1050) | copy-start | bytes 772 | tf_op jit(solution)/shard_map/while
  663.4 38.9 %copy-start.71 = (bf16[128]{0:T(256)(128)(2,1)S(1)}, bf16[128]{0:T(256)(128)(2,1)}, u32[]{:S(2)}) copy-start(bf16[128]{0:T(256)(128)(2,1)} %get-tuple-element.1056) | copy-start | bytes 772 | tf_op jit(solution)/shard_map/while
  663.4 55.8 %copy-start.72 = (bf16[128]{0:T(256)(128)(2,1)S(1)}, bf16[128]{0:T(256)(128)(2,1)}, u32[]{:S(2)}) copy-start(bf16[128]{0:T(256)(128)(2,1)} %get-tuple-element.1057) | copy-start | bytes 772 | tf_op jit(solution)/shard_map/while
  663.4 74.8 %copy-start.73 = (bf16[128]{0:T(256)(128)(2,1)S(1)}, bf16[128]{0:T(256)(128)(2,1)}, u32[]{:S(2)}) copy-start(bf16[128]{0:T(256)(128)(2,1)} %get-tuple-element.1061) | copy-start | bytes 772 | tf_op jit(solution)/shard_map/while
  663.4 91.8 %copy-start.74 = (bf16[128]{0:T(256)(128)(2,1)S(1)}, bf16[128]{0:T(256)(128)(2,1)}, u32[]{:S(2)}) copy-start(bf16[128]{0:T(256)(128)(2,1)} %get-tuple-element.1062) | copy-start | bytes 772 | tf_op jit(solution)/shard_map/while
  663.4 170.0 %all-gather.53.cloned.1.call-start = ((), (), s32[]{:S(2)}) async-start(), calls=%async_computation.9 | async-start | bytes 2359296 | tf_op jit(solution)/shard_map/while/body/eval_jaxpr/all_gather | solution.py:260
  664.0 175.4 %all-gather.55.cloned.1.call-start = ((), (), s32[]{:S(2)}) async-start(), calls=%async_computation.10 | async-start | bytes 7077888 | tf_op jit(solution)/shard_map/while/body/eval_jaxpr/all_gather | solution.py:243
  664.6 485.8 %all-gather.57.cloned.1.call-start = ((), (), s32[]{:S(2)}) async-start(), calls=%async_computation.11 | async-start | bytes 9437184 | tf_op jit(solution)/shard_map/while/body/eval_jaxpr/all_gather | solution.py:247
  665.4 536.3 %all-gather.59.cloned.1.call-start = ((), (), s32[]{:S(2)}) async-start(), calls=%async_computation.12 | async-start | bytes 9437184 | tf_op jit(solution)/shard_map/while/body/eval_jaxpr/all_gather | solution.py:264
  667.7 171.7 %copy-start.35 = (f32[1024]{0:T(1024)}, f32[1024]{0:T(1024)S(1)}, u32[]{:S(2)}) copy-start(f32[1024]{0:T(1024)S(1)} %fusion.198) | copy-start | bytes 12292 | tf_op jit(solution)/shard_map/while
  684.0 155.4 %copy-start.32 = (f32[8,1,128]{2,1,0:T(1,128)}, f32[8,1,128]{2,1,0:T(1,128)S(1)}, u32[]{:S(2)}) copy-start(f32[8,1,128]{2,1,0:T(1,128)S(1)} %convert_element_type.636) | copy-start | bytes 12292 | tf_op jit(solution)/shard_map/while
  702.3 137.2 %copy-start.63 = (f32[8,1,128]{2,1,0:T(1,128)}, f32[8,1,128]{2,1,0:T(1,128)S(1)}, u32[]{:S(2)}) copy-start(f32[8,1,128]{2,1,0:T(1,128)S(1)} %convert_element_type.635) | copy-start | bytes 12292 | tf_op jit(solution)/shard_map/while
  776.0 63.5 %copy-start.17 = (f32[1024]{0:T(1024)}, f32[1024]{0:T(1024)S(1)}, u32[]{:S(2)}) copy-start(f32[1024]{0:T(1024)S(1)} %broadcast_multiply_fusion.2) | copy-start | bytes 12292 | tf_op jit(solution)/shard_map/while
  779.4 53.7 %copy-start.30 = (f32[1024]{0:T(1024)}, f32[1024]{0:T(1024)S(1)}, u32[]{:S(2)}) copy-start(f32[1024]{0:T(1024)S(1)} %get-tuple-element.929) | copy-start | bytes 12292 | tf_op jit(solution)/shard_map/while
  779.4 60.1 %copy-start.20 = (f32[1024]{0:T(1024)}, f32[1024]{0:T(1024)S(1)}, u32[]{:S(2)}) copy-start(f32[1024]{0:T(1024)S(1)} %fusion.200) | copy-start | bytes 12292 | tf_op jit(solution)/shard_map/while
  833.3 37.2 %copy-start.23 = (f32[1024,8]{0,1:T(8,128)}, f32[1024,8]{0,1:T(8,128)S(1)}, u32[]{:S(2)}) copy-start(f32[1024,8]{0,1:T(8,128)S(1)} %get-tuple-element.933) | copy-start | bytes 98308 | tf_op jit(solution)/shard_map/while
  833.3 37.2 %copy-start.25 = (f32[1024,8]{0,1:T(8,128)}, f32[1024,8]{0,1:T(8,128)S(1)}, u32[]{:S(2)}) copy-start(f32[1024,8]{0,1:T(8,128)S(1)} %get-tuple-element.932) | copy-start | bytes 98308 | tf_op jit(solution)/shard_map/while
  870.5 26.0 %copy-start = (f32[1024,16,48]{0,2,1:T(8,128)}, f32[1024,16,48]{0,2,1:T(8,128)S(1)}, u32[]{:S(2)}) copy-start(f32[1024,16,48]{0,2,1:T(8,128)S(1)} %slice.108) | copy-start | bytes 9437188 | tf_op jit(solution)/shard_map/while
  872.0 24.6 %copy-start.7 = (f32[1024,16,8]{0,2,1:T(8,128)}, f32[1024,16,8]{0,2,1:T(8,128)S(1)}, u32[]{:S(2)}) copy-start(f32[1024,16,8]{0,2,1:T(8,128)S(1)} %get-tuple-element.937) | copy-start | bytes 1572868 | tf_op jit(solution)/shard_map/while
  872.0 24.6 %copy-start.9 = (f32[1024,16,8]{0,2,1:T(8,128)}, f32[1024,16,8]{0,2,1:T(8,128)S(1)}, u32[]{:S(2)}) copy-start(f32[1024,16,8]{0,2,1:T(8,128)S(1)} %get-tuple-element.936) | copy-start | bytes 1572868 | tf_op jit(solution)/shard_map/while
  872.0 24.6 %copy-start.13 = (bf16[1024,16,8]{0,2,1:T(8,128)(2,1)}, bf16[1024,16,8]{0,2,1:T(8,128)(2,1)S(1)}, u32[]{:S(2)}) copy-start(bf16[1024,16,8]{0,2,1:T(8,128)(2,1)S(1)} %get-tuple-element.934) | copy-start | bytes 786436 | tf_op jit(solution)/shard_map/while
  918.5 27.1 %copy-start.12 = (bf16[1024,1024]{0,1:T(8,128)(2,1)S(1)}, bf16[1024,1024]{0,1:T(8,128)(2,1)}, u32[]{:S(2)}) copy-start(bf16[1024,1024]{0,1:T(8,128)(2,1)} %convolution_convert_fusion.2) | copy-start | bytes 6291460 | tf_op jit(solution)/shard_map/while
  1020.8 54.4 %copy-start.8 = (f32[1024,16,8]{0,2,1:T(8,128)S(1)}, f32[1024,16,8]{0,2,1:T(8,128)}, u32[]{:S(2)}) copy-start(f32[1024,16,8]{0,2,1:T(8,128)} %copy-done.7) | copy-start | bytes 1572868 | tf_op jit(solution)/shard_map/while
  1020.8 54.4 %copy-start.10 = (f32[1024,16,8]{0,2,1:T(8,128)S(1)}, f32[1024,16,8]{0,2,1:T(8,128)}, u32[]{:S(2)}) copy-start(f32[1024,16,8]{0,2,1:T(8,128)} %copy-done.9) | copy-start | bytes 1572868 | tf_op jit(solution)/shard_map/while
  1150.5 51.2 %copy-start.37 = (f32[1024]{0:T(1024)S(1)}, f32[1024]{0:T(1024)}, u32[]{:S(2)}) copy-start(f32[1024]{0:T(1024)} %copy-done.35) | copy-start | bytes 12292 | tf_op jit(solution)/shard_map/while
  1322.5 69.5 %reduce-scatter.7.cloned.1.call-start = ((), (), s32[]{:S(2)}) async-start(), calls=%async_computation.5 | async-start | bytes 2359296 | tf_op jit(solution)/shard_map/reduce_scatter | solution.py:283
  1326.4 185.6 %reduce-scatter.5.cloned.1.call-start = ((), (), s32[]{:S(2)}) async-start(), calls=%async_computation.4 | async-start | bytes 7077888 | tf_op jit(solution)/shard_map/reduce_scatter | solution.py:283
  1334.7 327.2 %reduce-scatter.9.cloned.1.call-start = ((), (), s32[]{:S(2)}) async-start(), calls=%async_computation.6 | async-start | bytes 9437184 | tf_op jit(solution)/shard_map/reduce_scatter | solution.py:283
  1343.9 468.2 %reduce-scatter.11.cloned.1.call-start = ((), (), s32[]{:S(2)}) async-start(), calls=%async_computation.7 | async-start | bytes 9437184 | tf_op jit(solution)/shard_map/reduce_scatter | solution.py:283
  1353.2 458.9 %copy-start.80 = (u32[32]{0:T(128)S(1)}, u32[32]{0:T(128)}, u32[]{:S(2)}) copy-start(u32[32]{0:T(128)} %constant.127) | copy-start | bytes 388
  1353.2 461.5 %copy-start.56 = (f32[1024]{0:T(1024)S(1)}, f32[1024]{0:T(1024)}, u32[]{:S(2)}) copy-start(f32[1024]{0:T(1024)} %get-tuple-element.246) | copy-start | bytes 12292
  1353.2 461.5 %copy-start.53 = (f32[1024]{0:T(1024)S(1)}, f32[1024]{0:T(1024)}, u32[]{:S(2)}) copy-start(f32[1024]{0:T(1024)} %get-tuple-element.247) | copy-start | bytes 12292
  1353.2 461.5 %copy-start.50 = (f32[1024]{0:T(1024)S(1)}, f32[1024]{0:T(1024)}, u32[]{:S(2)}) copy-start(f32[1024]{0:T(1024)} %get-tuple-element.248) | copy-start | bytes 12292
  1353.2 461.5 %copy-start.47 = (f32[1024]{0:T(1024)S(1)}, f32[1024]{0:T(1024)}, u32[]{:S(2)}) copy-start(f32[1024]{0:T(1024)} %get-tuple-element.249) | copy-start | bytes 12292
  1353.2 461.6 %copy-start.43 = (f32[3072]{0:T(1024)S(1)}, f32[3072]{0:T(1024)}, u32[]{:S(2)}) copy-start(f32[3072]{0:T(1024)} %get-tuple-element.239) | copy-start | bytes 36868
  1353.2 461.6 %copy-start.40 = (f32[4096]{0:T(1024)S(1)}, f32[4096]{0:T(1024)}, u32[]{:S(2)}) copy-start(f32[4096]{0:T(1024)} %get-tuple-element.243) | copy-start | bytes 49156
  1353.2 529.4 %all-reduce.19.cloned.1.call-start = ((), (), s32[]{:S(2)}) async-start(), calls=%async_computation.8 | async-start | bytes 6291456 | tf_op jit(solution)/shard_map/psum | solution.py:285
  (109 other events, 923.7 us)
Sparse Core Ops, SparseCore 0:
  11.8 52.0 all-gather.52
  66.0 97.8 all-gather.54
  166.1 123.3 all-gather.56
  291.5 123.0 all-gather.58
  666.1 46.4 all-gather.52
  714.6 97.8 all-gather.54
  814.6 123.2 all-gather.56
  940.0 123.1 all-gather.58
Sparse Core Ops, SparseCore 1:
  1327.1 64.8 reduce-scatter.6
  1395.4 116.6 reduce-scatter.4
  1515.6 146.2 reduce-scatter.8
  1665.9 146.1 reduce-scatter.10
  1814.7 67.9 all-reduce.18
where the time goes:
time: 1900 us
  matrix products  715 us (38%)
  waiting for transfers between devices  486 us (26%)
  blocking collectives  359 us (19%)
  other arithmetic  252 us (13%)
  local copies, waits for them, and re-layouts  62.7 us (3%)
    reduce_scatter x4, waiting for transfers between devices, body(): lax.psum_scatter(as_sent(carry), 'fsdp', scatter_dimension=0, tiled=True)  459 us
    convert_element_type x2, other arithmetic, backward(): grad_scores = grad_scores.astype(jnp.bfloat16)  109 us
    dot_general x2, matrix products, forward(): jnp.dot(second, up_weight, preferred_element_type=jnp.float32)  102 us
    dot_general x2, matrix products, backward(): jnp.einsum('qhd,khd->hqk', grad_context, values, preferred_element_type=j...  97.2 us
    dot_general x2, matrix products, forward(): jnp.einsum('hqk,khd->qhd', probs.astype(jnp.bfloat16), values, preferred_...  54 us
    dot_general x2, matrix products, backward(): jnp.einsum('hqk,qhd->khd', probs.astype(jnp.bfloat16), grad_context, pref...  53.4 us
    all_gather x2, blocking collectives, micro(): lax.all_gather(shards[1], 'fsdp', axis=0, tiled=True)  53 us
    all_gather x2, blocking collectives, micro(): lax.all_gather(shards[5], 'fsdp', axis=0, tiled=True)  52.9 us
  transfers between devices with their start and end apart: 13, of which 5 were waited for; matrix products, arithmetic and copies ran while one was open for 41% of the time, Pallas kernels for 0%

commit v1 on v0

v1 whole, which is shorter than its diff:
```python
import math

import jax
import jax.numpy as jnp
from jax import lax
from jax.experimental import pallas as pl
from jax.experimental.pallas import tpu as pltpu
from jax.sharding import PartitionSpec as P

HEADS = 16
HEAD = 64
ROT = 16
PAIR = 2 * HEAD
GROUPS = 2
QTILE = 256
VMEM = 48 * 1024 * 1024
EPS = 1e-05
BASE = 10000.0
F32 = jnp.float32
BF16 = jnp.bfloat16


def dot_nn(a, b):
    return lax.dot_general(a, b, (((1,), (0,)), ((), ())), preferred_element_type=F32)


def dot_nt(a, b):
    return lax.dot_general(a, b, (((1,), (1,)), ((), ())), preferred_element_type=F32)


def dot_tn(a, b):
    return lax.dot_general(a, b, (((0,), (0,)), ((), ())), preferred_element_type=F32)


def rotary_tables(rows):
    half = ROT // 2
    lane = jnp.arange(PAIR, dtype=jnp.int32) % HEAD
    steps = (lane % half).astype(F32) * (2.0 / ROT)
    inverse = jnp.exp(-math.log(BASE) * steps)
    angles = jnp.arange(rows, dtype=F32)[:, None] * inverse[None, :]
    cosines = jnp.where(lane[None] < ROT, jnp.cos(angles), 1.0)
    ahead = jnp.where(lane[None] < half, -jnp.sin(angles), 0.0)
    behind = jnp.where((lane[None] >= half) & (lane[None] < ROT), jnp.sin(angles), 0.0)
    return cosines, ahead, behind


def mlp_kernel(second, outer, up, up_bias, down, active, grad_hidden):
    hidden = dot_nn(second[...], up[...]) + up_bias[...].astype(F32)
    grad_active = dot_nt(outer[...], down[...])
    below = 0.5 + 0.5 * lax.erf(hidden * (0.5**0.5))
    density = jnp.exp(-0.5 * hidden * hidden) * (1.0 / math.sqrt(2.0 * math.pi))
    active[...] = (hidden * below).astype(BF16)
    grad_hidden[...] = (grad_active * (below + hidden * density)).astype(BF16)


def mlp_front(second, outer, up, up_bias, down):
    rows, width = second.shape
    wide = up.shape[1]
    rt, ft = min(512, rows), min(512, wide)
    out = jax.ShapeDtypeStruct((rows, wide), BF16)
    return pl.pallas_call(
        mlp_kernel,
        grid=(wide // ft, rows // rt),
        in_specs=[
            pl.BlockSpec((rt, width), lambda f, r: (r, 0)),
            pl.BlockSpec((rt, width), lambda f, r: (r, 0)),
            pl.BlockSpec((width, ft), lambda f, r: (0, f)),
            pl.BlockSpec((1, ft), lambda f, r: (0, f)),
            pl.BlockSpec((ft, width), lambda f, r: (f, 0)),
        ],
        out_specs=[pl.BlockSpec((rt, ft), lambda f, r: (r, f))] * 2,
        out_shape=[out, out],
        compiler_params=pltpu.CompilerParams(vmem_limit_bytes=VMEM),
        cost_estimate=pl.CostEstimate(
            flops=4 * rows * width * wide,
            bytes_accessed=rows * wide * 4 + width * wide * 4 + rows * width * 32,
            transcendentals=2 * rows * wide,
        ),
    )(second, outer, up, up_bias.reshape(1, wide), down)


def attention_kernel(qin, kin, vin, gin, cosines, ahead, behind, context, gq, gk, gv, acc_k, acc_v):
    rows = qin.shape[1]
    cos, s1, s2 = cosines[...], ahead[...], behind[...]

    def turn(u):
        return u * cos + pltpu.roll(u, PAIR - ROT // 2, 1) * s1 + pltpu.roll(u, ROT // 2, 1) * s2

    def back(u, c, a, b):
        return u * c - pltpu.roll(u, PAIR - ROT // 2, 1) * a - pltpu.roll(u, ROT // 2, 1) * b

    query = (turn(qin[0]) * HEAD ** (-0.5)).astype(BF16)
    keys = turn(kin[0]).astype(BF16)
    values = vin[0].astype(BF16)
    grad = gin[0]
    lane = lax.broadcasted_iota(jnp.int32, (1, PAIR), 1)
    causal = lax.broadcasted_iota(jnp.int32, (QTILE, QTILE), 0) >= lax.broadcasted_iota(
        jnp.int32, (QTILE, QTILE), 1
    )
    zero = jnp.zeros((), BF16)
    halves = [(lane < HEAD), (lane >= HEAD)]
    query_h = [jnp.where(m, query, zero) for m in halves]
    keys_h = [jnp.where(m, keys, zero) for m in halves]
    values_h = [jnp.where(m, values, zero) for m in halves]
    grad_h = [jnp.where(m, grad, zero) for m in halves]
    acc_k[...] = jnp.zeros_like(acc_k)
    acc_v[...] = jnp.zeros_like(acc_v)
    for tile in range(rows // QTILE):
        low, high = tile * QTILE, (tile + 1) * QTILE
        ctx = jnp.zeros((QTILE, PAIR), F32)
        dq = jnp.zeros((QTILE, PAIR), F32)
        for h in range(2):
            q, g = query_h[h][low:high], grad_h[h][low:high]
            scores = dot_nt(q, keys[:high])
            last = jnp.where(causal, scores[:, low:], -1e30)
            scores = last if tile == 0 else jnp.concatenate([scores[:, :low], last], axis=1)
            peak = jnp.max(scores, axis=1, keepdims=True)
            expo = jnp.exp(scores - peak)
            probs = expo * (1.0 / jnp.sum(expo, axis=1, keepdims=True))
            low_probs = probs.astype(BF16)
            ctx += dot_nn(low_probs, values_h[h][:high])
            grad_probs = dot_nt(g, values[:high])
            inner = jnp.sum(probs * grad_probs, axis=1, keepdims=True)
            grad_scores = (probs * (grad_probs - inner)).astype(BF16)
            dq += dot_nn(grad_scores, keys_h[h][:high])
            acc_k[:high] += dot_tn(grad_scores, q)
            acc_v[:high] += dot_tn(low_probs, g)
        context[0, low:high] = ctx.astype(BF16)
        dq = back(dq * HEAD ** (-0.5), cos[low:high], s1[low:high], s2[low:high])
        gq[0, low:high] = dq.astype(BF16)
    gk[0] = back(acc_k[...], cos, s1, s2).astype(BF16)
    gv[0] = acc_v[...].astype(BF16)


def attention(mixed, grad_context, tables, group, groups):
    batch, rows, width = grad_context.shape
    pairs = width // PAIR
    each = pairs // groups
    start = group * each
    out = jax.ShapeDtypeStruct((batch, rows, each * PAIR), BF16)

    def at(offset):
        return pl.BlockSpec((1, rows, PAIR), lambda b, p: (b, 0, offset + p))

    table = pl.BlockSpec((rows, PAIR), lambda b, p: (0, 0))
    steps = batch * each
    return pl.pallas_call(
        attention_kernel,
        grid=(batch, each),
        in_specs=[at(start), at(pairs + start), at(2 * pairs + start), at(start)] + [table] * 3,
        out_specs=[at(0)] * 4,
        out_shape=[out] * 4,
        scratch_shapes=[pltpu.VMEM((rows, PAIR), F32)] * 2,
        compiler_params=pltpu.CompilerParams(vmem_limit_bytes=VMEM),
        cost_estimate=pl.CostEstimate(
            flops=steps * 24 * rows * rows * PAIR,
            bytes_accessed=steps * rows * PAIR * 22,
            transcendentals=steps * 2 * rows * rows,
        ),
    )(mixed, mixed, mixed, grad_context, *tables)


def reduce_owner(total):
    copies, owners = lax.axis_size("rep"), lax.axis_size("fsdp")
    core = lax.axis_index("rep") % 2
    half = total.shape[0] // (2 * owners)
    columns = total.shape[1]
    parts = total.reshape(owners, 2, half, columns)
    theirs = lax.dynamic_index_in_dim(parts, 1 - core, 1, keepdims=False).astype(BF16)
    mine = lax.dynamic_index_in_dim(parts, core, 1, keepdims=False)
    got = lax.ppermute(theirs, "rep", [(i, i ^ 1) for i in range(copies)])
    pair = (mine + got.astype(F32)).astype(BF16).reshape(owners * half, columns)
    owned = lax.psum_scatter(pair, "fsdp", scatter_dimension=0, tiled=True)
    every = lax.all_gather(owned, "rep", axis=0, tiled=False).astype(F32)
    every = every.reshape(copies // 2, 2, half, columns)
    return jnp.sum(every, axis=0).reshape(2 * half, columns)


def body(
    tokens,
    lengths,
    cotangent,
    mix_weight,
    mix_bias,
    proj_weight,
    proj_bias,
    up_weight,
    up_bias,
    down_weight,
    down_bias,
    gain_attn,
    shift_attn,
    gain_mlp,
    shift_mlp,
):
    owners = lax.axis_size("fsdp")
    batch, rows, width = tokens.shape
    count = batch * rows
    small = (gain_mlp, shift_mlp, up_bias, gain_attn, shift_attn, mix_bias, proj_bias, down_bias)
    sizes = [piece.shape[0] for piece in small]
    packed = lax.all_gather(jnp.concatenate(small), "fsdp", axis=0, tiled=False)
    pieces, at = [], 0
    for size in sizes:
        pieces.append(packed[:, at : at + size].reshape(owners * size))
        at += size
    gain_mlp, shift_mlp, up_bias, gain_attn, shift_attn, mix_bias, proj_bias, down_bias = pieces
    up_full = lax.all_gather(up_weight, "fsdp", axis=0, tiled=True)
    down_full = lax.all_gather(down_weight, "fsdp", axis=0, tiled=True)
    proj_full = lax.all_gather(proj_weight, "fsdp", axis=0, tiled=True)
    mix_full = lax.all_gather(mix_weight, "fsdp", axis=0, tiled=True)

    places = jnp.arange(rows, dtype=jnp.int32)
    valid = (places[None, :] < lengths[:, None]).reshape(count, 1)
    inputs = tokens.reshape(count, width).astype(F32)
    outer = jnp.where(valid, cotangent.reshape(count, width), jnp.zeros((), BF16))
    mean = jnp.mean(inputs, axis=1, keepdims=True)
    centred = inputs - mean
    scale = lax.rsqrt(jnp.mean(centred * centred, axis=1, keepdims=True) + EPS)
    hat = centred * scale
    g_attn, g_mlp = gain_attn.astype(F32), gain_mlp.astype(F32)
    first = (hat * g_attn + shift_attn.astype(F32)).astype(BF16)
    second = (hat * g_mlp + shift_mlp.astype(F32)).astype(BF16)

    active, grad_hidden = mlp_front(second, outer, up_full, up_bias, down_full)
    grad_down = reduce_owner(dot_tn(active, outer))
    grad_up = reduce_owner(dot_tn(second, grad_hidden))
    grad_second = dot_nt(grad_hidden, up_full)
    feed = dot_nn(active, down_full)

    mixed = (dot_nn(first, mix_full) + mix_bias.astype(F32)).reshape(batch, rows, 3 * width)
    grad_context = dot_nt(outer, proj_full).astype(BF16).reshape(batch, rows, width)
    tables = rotary_tables(rows)
    share = width // GROUPS
    contexts, grads, mix_grads = [], [[], [], []], []
    for group in range(GROUPS):
        context, *three = attention(mixed, grad_context, tables, group, GROUPS)
        three = [piece.reshape(count, share) for piece in three]
        contexts.append(context.reshape(count, share))
        for kind in range(3):
            grads[kind].append(three[kind])
        own = reduce_owner(dot_tn(first, jnp.concatenate(three, axis=1)))
        mix_grads.append(own.reshape(-1, 3, share))
    grad_mix = jnp.stack(mix_grads, axis=2).reshape(-1, 3 * width)
    context = jnp.concatenate(contexts, axis=1)
    grad_mixed = jnp.concatenate(grads[0] + grads[1] + grads[2], axis=1)
    grad_proj = reduce_owner(dot_tn(context, outer))
    attend = dot_nn(context, proj_full)
    result = inputs + attend + feed + (proj_bias.astype(F32) + down_bias.astype(F32))
    result = jnp.where(valid, result, 0.0).astype(BF16)
    grad_first = dot_nt(grad_mixed, mix_full)

    pulled = grad_first * g_attn + grad_second * g_mlp
    into = scale * (
        pulled
        - jnp.mean(pulled, axis=1, keepdims=True)
        - hat * jnp.mean(pulled * hat, axis=1, keepdims=True)
    )
    grad_tokens = outer.astype(F32) + into

    def over_rows(array):
        return jnp.sum(array.astype(F32), axis=0)

    vectors = (
        over_rows(grad_second * hat),
        over_rows(grad_second),
        over_rows(grad_hidden),
        over_rows(grad_first * hat),
        over_rows(grad_first),
        over_rows(grad_mixed),
        over_rows(outer),
    )
    sent = jnp.concatenate([piece.reshape(owners, -1) for piece in vectors], axis=1)
    sent = lax.psum_scatter(sent.astype(BF16), "fsdp", scatter_dimension=0, tiled=True)
    owned = jnp.sum(lax.all_gather(sent[0], "rep", axis=0, tiled=False).astype(F32), axis=0)
    pieces, at = [], 0
    for size in sizes[:7]:
        pieces.append(owned[at : at + size])
        at += size
    d_gain_mlp, d_shift_mlp, d_up_bias, d_gain_attn, d_shift_attn, d_mix_bias, d_bias = pieces
    return (
        result.reshape(batch, rows, width),
        grad_tokens.reshape(batch, rows, width),
        grad_mix,
        d_mix_bias,
        grad_proj,
        d_bias,
        grad_up,
        d_up_bias,
        grad_down,
        d_bias,
        d_gain_attn,
        d_shift_attn,
        d_gain_mlp,
        d_shift_mlp,
    )


def solution(mesh):
    in_specs = (
        P(("rep", "fsdp"), None, None),
        P(("rep", "fsdp")),
        P(("rep", "fsdp"), None, None),
        P("fsdp", None),
        P("fsdp"),
        P("fsdp", None),
        P("fsdp"),
        P("fsdp", None),
        P("fsdp"),
        P("fsdp", None),
        P("fsdp"),
        P("fsdp"),
        P("fsdp"),
        P("fsdp"),
        P("fsdp"),
    )
    out_specs = (
        P(("rep", "fsdp"), None, None),
        P(("rep", "fsdp"), None, None),
        P("fsdp", None),
        P("fsdp"),
        P("fsdp", None),
        P("fsdp"),
        P("fsdp", None),
        P("fsdp"),
        P("fsdp", None),
        P("fsdp"),
        P("fsdp"),
        P("fsdp"),
        P("fsdp"),
        P("fsdp"),
    )
    return jax.shard_map(body, mesh=mesh, in_specs=in_specs, out_specs=out_specs, check_vma=False)
```

time: 1900 us -> 978 us (0.51)
  matrix products: 715 us -> 189 us
  blocking collectives: 359 us -> 98.9 us
  Pallas kernels: 0 us -> 192 us
  waiting for transfers between devices: 486 us -> 302 us
  other arithmetic: 252 us -> 82.2 us
  local copies, waits for them, and re-layouts: 62.7 us -> 92 us
    dot_general x36 -> x11, matrix products: 715 us -> 189 us  [the longest x5 73.4 us: dot_tn(): lax.dot_general(a, b, (((0,), (0,)), ((), ())), preferred_element_type=F32)]
    reduce_scatter x4 -> x5, waiting for transfers between devices: 459 us -> 101 us  [reduce_owner(): owned = lax.psum_scatter(pair, 'fsdp', scatter_dimension=0, tiled=True)]
    all_gather x16 -> x5, blocking collectives: 318 us -> 63.5 us  [the longest x1 32.9 us: body(): packed = lax.all_gather(jnp.concatenate(small), 'fsdp', axis=0, tiled=False)]
    pallas_call x0 -> x3, Pallas kernels: none -> 192 us  [the longest x2 141 us: attention(): pl.pallas_call(attention_kernel, grid=(batch, each), in_specs=[at(start),...]
    all_gather x8 -> x6, waiting for transfers between devices: 0.09 us -> 188 us  [the longest x1 81.4 us: body(): mix_full = lax.all_gather(mix_weight, 'fsdp', axis=0, tiled=True)]
    convert_element_type x44 -> x8, other arithmetic: 159 us -> 28.1 us  [the longest x5 23.5 us: reduce_owner(): pair = (mine + got.astype(F32)).astype(BF16).reshape(owners * half, columns)]
    dot_general x0 -> x4, local copies, waits for them, and re-layouts: none -> 42.1 us  [dot_tn(): lax.dot_general(a, b, (((0,), (0,)), ((), ())), preferred_element_type=F32)]
    reduce_sum x10 -> x11, other arithmetic: 70.1 us -> 33.1 us  [the longest x3 20.5 us: over_rows(): return jnp.sum(array.astype(F32), axis=0)]
  transfers between devices with their start and end apart: 13 -> 16, of which waited for: 5 -> 8; matrix products, arithmetic and copies ran while one was open for 41% -> 31% of each run, Pallas kernels for 0% -> 15%
where the time goes in v1:
time: 978 us; the launch traced here: 973 us
  waiting for transfers between devices  302 us (31%)
  Pallas kernels  192 us (20%)
  matrix products  189 us (19%)
  blocking collectives  98.9 us (10%)
  local copies, waits for them, and re-layouts  92 us (9%)
  other arithmetic  82.2 us (8%)
  between operations  14.7 us (2%)
    pallas_call x2, Pallas kernels, attention(): pl.pallas_call(attention_kernel, grid=(batch, each), in_specs=[at(start),...  141 us
    reduce_scatter x5, waiting for transfers between devices, reduce_owner(): owned = lax.psum_scatter(pair, 'fsdp', scatter_dimension=0, tiled=True)  101 us
    all_gather x1, waiting for transfers between devices, body(): mix_full = lax.all_gather(mix_weight, 'fsdp', axis=0, tiled=True)  81.4 us
    all_gather x1, waiting for transfers between devices, body(): down_full = lax.all_gather(down_weight, 'fsdp', axis=0, tiled=True)  77.4 us
    dot_general x5, matrix products, dot_tn(): lax.dot_general(a, b, (((0,), (0,)), ((), ())), preferred_element_type=F32)  73.4 us
    dot_general x3, matrix products, dot_nt(): lax.dot_general(a, b, (((1,), (1,)), ((), ())), preferred_element_type=F32)  58.9 us
    dot_general x3, matrix products, dot_nn(): lax.dot_general(a, b, (((1,), (0,)), ((), ())), preferred_element_type=F32)  57 us
    pallas_call x1, Pallas kernels, mlp_front(): pl.pallas_call(mlp_kernel, grid=(wide // ft, rows // rt), in_specs=[pl.Bl...  51.1 us
  transfers between devices with their start and end apart: 16, of which 8 were waited for; matrix products, arithmetic and copies ran while one was open for 31% of the time, Pallas kernels for 15%

profile of v1, /device:TPU:0, one launch (start us, length us, event | category | flops | bytes accessed | tf_op | source)
XLA Modules:
  0.0 972.9 jit_solution(6438889983946527956)
XLA Ops:
  17.5 3.0 convert_reduce_fusion
  21.1 1.4 fusion.5
  22.6 32.9 %all-gather.6 = bf16[8,1,1664]{2,1,0:T(2,128)(2,1)S(1)} all-gather(bf16[1,1,1664]{2,1,0:T(2,128)(2,1)S(1)} %reshape.412), channel_id=2, replica_groups=mesh['rep'=4,'fsdp'=8] {'fsdp'}, dimensions={0}, use_global_device_ids=true | all-gather | bytes 29952 | tf_op jit(solution)/shard_map/all_gather | solution.py:201
  55.6 2.8 fusion.48
  58.4 4.7 fusion.64
  63.1 2.7 bitcast_select_fusion.outer
  66.8 4.5 fusion.16
  71.3 9.7 convolution_convert_fusion
  81.0 81.4 %all-gather.15.cloned.1.call-done = bf16[1024,3072]{1,0:T(8,128)(2,1)} async-done(((bf16[128,3072]{1,0:T(8,128)(2,1)}), bf16[1024,3072]{1,0:T(8,128)(2,1)}) %all-gather.15.cloned.1.call-update) | async-done | bytes 6291472 | tf_op jit(solution)/shard_map/all_gather | solution.py:210
  162.4 19.9 %convolution_add_fusion = f32[2048,3072]{1,0:T(8,128)} fusion(bf16[2048,1024]{1,0:T(8,128)(2,1)} %get-tuple-element.49, bf16[1024,3072]{1,0:T(8,128)(2,1)} %all-gather.15.cloned.1.call-done, f32[3072]{0:T(1024)S(1)} %reshape.378), kind=kOutput, calls=%fused_computation.2 | convolution fusion | flops 12891193344 | bytes 35663872 | tf_op jit(solution)/shard_map/dot_general | solution.py:24
  182.4 70.4 %shard_map.255 = (bf16[2,1024,512]{2,1,0:T(8,128)(2,1)S(1)}, bf16[2,1024,512]{2,1,0:T(8,128)(2,1)S(1)}, bf16[2,1024,512]{2,1,0:T(8,128)(2,1)}, bf16[2,1024,512]{2,1,0:T(8,128)(2,1)}) custom-call(f32[2,1024,3072]{2,1,0:T(8,128)} %bitcast.259, f32[2,1024,3072]{2,1,0:T(8,128)} %bitcast.260, f32[2,1024,3072]{2,1,0:T(8,128)} %bitcast.261, ...), custom_call_target="tpu_custom_call" | custom-call | flops 25769803776 | bytes 23068672 | tf_op jit(solution)/shard_map/pallas_call | solution.py:147
  252.7 70.9 %shard_map.254 = (bf16[2,1024,512]{2,1,0:T(8,128)(2,1)S(1)}, bf16[2,1024,512]{2,1,0:T(8,128)(2,1)S(1)}, bf16[2,1024,512]{2,1,0:T(8,128)(2,1)}, bf16[2,1024,512]{2,1,0:T(8,128)(2,1)}) custom-call(f32[2,1024,3072]{2,1,0:T(8,128)} %bitcast.262, f32[2,1024,3072]{2,1,0:T(8,128)} %bitcast.263, f32[2,1024,3072]{2,1,0:T(8,128)} %bitcast.264, ...), custom_call_target="tpu_custom_call" | custom-call | flops 25769803776 | bytes 23068672 | tf_op jit(solution)/shard_map/pallas_call | solution.py:147
  323.6 1.3 copy-done.1
  324.9 1.4 copy-done.5
  326.3 2.6 fusion.41
  328.9 6.5 copy.43
  335.4 77.4 %all-gather.21.cloned.1.call-done.down = bf16[4096,1024]{1,0:T(8,128)(2,1)} async-done(((bf16[512,1024]{1,0:T(8,128)(2,1)}), bf16[4096,1024]{1,0:T(8,128)(2,1)}) %all-gather.21.cloned.1.call-update) | async-done | bytes 8388624 | tf_op jit(solution)/shard_map/all_gather | solution.py:208
  412.8 2.2 copy-done
  415.0 51.1 %shard_map.256 = (bf16[2048,4096]{1,0:T(8,128)(2,1)}, bf16[2048,4096]{1,0:T(8,128)(2,1)}) custom-call(bf16[2048,1024]{1,0:T(8,128)(2,1)S(1)} %copy-done, bf16[2048,1024]{1,0:T(8,128)(2,1)} %bitcast_select_fusion.outer, bf16[1024,4096]{1,0:T(8,128)(2,1)} %all-gather.19.cloned.1.call-done.up, bf16[1,4096]{1,0:T(2,128)(2,1)S(1)} %bitcast.217, ...), custom_call_target="tpu_custom_call" | custom-call | flops 34359738368 | bytes 117440512 | tf_op jit(solution)/shard_map/pallas_call | solution.py:61
  466.1 22.5 %copy.50 = bf16[4096,2048]{1,0:T(8,128)(2,1)} copy(bf16[4096,2048]{0,1:T(8,128)(2,1)} %bitcast.221) | data formatting | bytes 33554432 | tf_op jit(solution)/shard_map/dot_general | solution.py:32
  488.6 21.6 %fusion.68 = f32[8,2,256,1024]{3,2,1,0:T(8,128)S(1)} fusion(bf16[8,2,256,2048]{3,2,1,0:T(8,128)(2,1)} %bitcast.222, bf16[2048,1024,1,1]{1,0,3,2:T(8,128)(2,1)} %bitcast.227), kind=kOutput, calls=%fused_computation.136 | convolution fusion | flops 17179869184 | bytes 37748736 | tf_op jit(solution)/shard_map/dot_general | solution.py:32
  510.2 3.1 fusion.38
  513.4 11.5 %fusion.67 = f32[8,2,64,1024]{3,2,1,0:T(8,128)S(1)} fusion(bf16[8,2,64,2048]{3,2,1,0:T(8,128)(2,1)} %bitcast.229, bf16[2048,1024,1,1]{1,0,3,2:T(8,128)(2,1)} %bitcast.228), kind=kOutput, calls=%fused_computation.135 | convolution fusion | flops 4294967296 | bytes 12582912 | tf_op jit(solution)/shard_map/dot_general | solution.py:32
  527.2 2.9 collective-permute-done.2
  530.1 2.9 fusion.43
  533.1 6.5 copy.44
  539.6 8.2 fusion.2
  547.9 21.6 %fusion = f32[8,2,64,4096]{3,2,1,0:T(8,128)S(1)} fusion(bf16[8,2,64,2048]{3,2,1,0:T(8,128)(2,1)} %bitcast.232, bf16[2048,4096]{1,0:T(8,128)(2,1)} %get-tuple-element.33), kind=kOutput, calls=%fused_computation | convolution fusion | flops 17179869184 | bytes 37748736 | tf_op jit(solution)/shard_map/dot_general | solution.py:32
  569.5 5.7 copy-done.11
  575.2 2.6 fusion.37
  578.1 7.2 collective-permute-done.3
  585.2 6.8 fusion.3
  592.1 6.6 copy.42
  599.3 9.8 %fusion.32 = f32[8,2,64,1536]{3,2,1,0:T(8,128)S(1)} fusion(bf16[8,2,64,2048]{3,2,1,0:T(8,128)(2,1)} %bitcast.230, bf16[2048,512]{1,0:T(8,128)(2,1)} %bitcast.236, bf16[2048,512]{1,0:T(8,128)(2,1)} %bitcast.238, bf16[2048,512]{1,0:T(8,128)(2,1)S(1)} %bitcast.209), kind=kOutput, calls=%fused_computation.44 | convolution fusion | flops 6461325312 | bytes 16777216 | tf_op jit(solution)/shard_map/dot_general | solution.py:32
  610.3 8.9 fusion.27
  619.2 1.6 fusion.39
  621.3 3.4 fusion.44
  625.1 3.4 constant_dynamic-update-slice_fusion.5
  628.5 1.6 constant_dynamic-update-slice_fusion.4
  630.1 1.5 constant_dynamic-update-slice_fusion.3
  631.6 1.6 constant_dynamic-update-slice_fusion.2
  633.2 1.6 constant_dynamic-update-slice_fusion.1
  634.8 1.6 constant_dynamic-update-slice_fusion
  636.4 6.8 reduce.4
  643.2 10.1 %fusion.42 = f32[2048,1024]{1,0:T(8,128)} fusion(bf16[1024,1024]{1,0:T(8,128)(2,1)} %all-gather.17.cloned.1.call-done, bf16[2048,512]{1,0:T(8,128)(2,1)S(1)} %bitcast.214, bf16[2048,512]{1,0:T(8,128)(2,1)} %bitcast.216), kind=kOutput, calls=%fused_computation.64 | convolution fusion | flops 4303355904 | bytes 14680064 | tf_op jit(solution)/shard_map/dot_general | solution.py:24
  653.4 4.0 fusion.40
  657.4 7.5 all-gather.3
  665.9 24.2 %fusion.66 = f32[2048,1024]{1,0:T(8,128)} fusion(bf16[2048,4096]{1,0:T(8,128)(2,1)} %get-tuple-element.33, bf16[1024,4096]{1,0:T(8,128)(2,1)} %all-gather.19.cloned.1.call-done.up), kind=kOutput, calls=%fused_computation.134 | convolution fusion | flops 17179869184 | bytes 33554432 | tf_op jit(solution)/shard_map/dot_general | solution.py:28
  690.0 25.0 %fusion.61 = (bf16[1024]{0:T(1024)(128)(2,1)S(1)}, bf16[1024]{0:T(1024)(128)(2,1)S(1)}, f32[2048]{0:T(1024)S(1)}, f32[2048]{0:T(1024)S(1)}, f32[2048,1024]{1,0:T...) fusion(f32[2048]{0:T(1024)S(1)} %bitcast.257, f32[2048]{0:T(1024)S(1)} %bitcast.254, ...), kind=kOutput, calls=%fused_computation.129 | convolution fusion | flops 12916350976 | bytes 39895040 | tf_op jit(solution)/shard_map/dot_general | solution.py:28
  715.1 9.0 reduce.3
  724.2 35.4 %all-reduce = bf16[8,1536]{1,0:T(8,128)(2,1)S(1)} all-reduce(bf16[8,1536]{1,0:T(8,128)(2,1)S(1)} %constant_dynamic-update-slice_fusion.6), channel_id=10, replica_groups=mesh['rep'=4,'fsdp'=8] {'fsdp'}, use_global_device_ids=true, to_apply=%region_15.16.clone | all-reduce | flops 12288 | bytes 49152
  760.3 5.2 all-gather.7
  765.6 27.0 %fusion.26 = bf16[2048,1024]{1,0:T(8,128)(2,1)} fusion(f32[2048,1024]{1,0:T(8,128)} %fusion.42, bf16[2,1024,1024]{2,1,0:T(8,128)(2,1)} %param.15, bf16[2048,4096]{1,0:T(8,128)(2,1)} %get-tuple-element.26, bf16[4096,1024]{1,0:T(8,128)(2,1)} %all-gather.21.cloned.1.call-done.down, f32[1024]{0:T(1024)S(1)} %add_bitcast_fusion, pred[2048]{0:T(1024)(128)(4,1)S(1)} %copy-done.26), kind=kOutput, calls=%fused_computation.33 | convolution fusion | flops 17192452096 | bytes 41949184 | tf_op jit(solution)/shard_map/dot_general | solution.py:24
  794.3 10.1 %fusion.20 = f32[2048,1024]{1,0:T(8,128)} fusion(bf16[2,1024,1024]{2,1,0:T(8,128)(2,1)} %param.15, f32[2048,1024]{1,0:T(8,128)} %get-tuple-element.45, f32[2048]{0:T(1024)S(1)} %broadcast_multiply_fusion, f32[2048]{0:T(1024)S(1)} %broadcast_multiply_fusion.1, f32[2048]{0:T(1024)S(1)} %bitcast.258, f32[2048]{0:T(1024)S(1)} %bitcast.255, ...), kind=kLoop, calls=%fused_computation.27 | loop fusion | flops 20971520 | bytes 25200640 | tf_op jit(solution)/shard_map/add | solution.py:258
  804.4 42.6 %reduce-scatter.8.cloned.1.call-done = bf16[64,1536]{1,0:T(8,128)(2,1)} async-done(((bf16[512,1536]{1,0:T(8,128)(2,1)}), bf16[64,1536]{1,0:T(8,128)(2,1)}) %reduce-scatter.8.cloned.1.call-update) | async-done | bytes 196624 | tf_op jit(solution)/shard_map/reduce_scatter | solution.py:173
  847.0 8.8 all-gather.2
  856.8 57.9 %reduce-scatter.6.cloned.1.call-done = bf16[64,1536]{1,0:T(8,128)(2,1)} async-done(((bf16[512,1536]{1,0:T(8,128)(2,1)}), bf16[64,1536]{1,0:T(8,128)(2,1)}) %reduce-scatter.6.cloned.1.call-update) | async-done | bytes 196624 | tf_op jit(solution)/shard_map/reduce_scatter | solution.py:173
  914.8 9.1 all-gather.1
  924.9 1.4 pad_maximum_fusion.2
  926.4 2.5 reshape.355
  928.9 9.0 all-gather.25.cloned.1.call-done
  937.8 3.6 convert_reduce_fusion.1
  941.4 20.7 %all-gather.23.cloned.1.call-done = bf16[256,4096]{1,0:T(8,128)(2,1)} async-done(((bf16[64,4096]{1,0:T(8,128)(2,1)}), bf16[256,4096]{1,0:T(8,128)(2,1)}) %all-gather.23.cloned.1.call-update) | async-done | bytes 2097168 | tf_op jit(solution)/shard_map/all_gather | solution.py:174
  962.1 3.5 convert_reduce_fusion.2
  (150 shorter events, 23.4 us)
Async XLA Ops:
  7.2 64.2 %all-gather.17.cloned.1.call-start = ((), (), s32[]{:S(2)}) async-start(), calls=%async_computation.6 | async-start | bytes 2359296 | tf_op jit(solution)/shard_map/all_gather | solution.py:209
  7.9 154.5 %all-gather.15.cloned.1.call-start = ((), (), s32[]{:S(2)}) async-start(), calls=%async_computation.5 | async-start | bytes 7077888 | tf_op jit(solution)/shard_map/all_gather | solution.py:210
  8.7 326.7 %all-gather.19.cloned.1.call-start = ((), (), s32[]{:S(2)}) async-start(), calls=%async_computation.7 | async-start | bytes 9437184 | tf_op jit(solution)/shard_map/all_gather | solution.py:207
  9.4 403.4 %all-gather.21.cloned.1.call-start = ((), (), s32[]{:S(2)}) async-start(), calls=%async_computation.8 | async-start | bytes 9437184 | tf_op jit(solution)/shard_map/all_gather | solution.py:208
  10.0 647.5 %reduce-scatter.10.cloned.1.call-start = ((), (), s32[]{:S(2)}) async-start(), calls=%async_computation.11 | async-start | bytes 1179648 | tf_op jit(solution)/shard_map/reduce_scatter | solution.py:173
  10.8 52.3 %copy-start.25 = (pred[2048]{0:T(1024)(128)(4,1)}, pred[2048]{0:T(1024)(128)(4,1)S(1)}, u32[]{:S(2)}) copy-start(pred[2048]{0:T(1024)(128)(4,1)S(1)} %lt.114) | copy-start | bytes 6148
  17.5 3.6 copy-start.7
  20.6 45.2 %copy-start.21 = (f32[1,8,2,128]{3,1,2,0:T(8,128)}, f32[1,8,2,128]{3,1,2,0:T(8,128)S(1)}, u32[]{:S(2)}) copy-start(f32[1,8,2,128]{3,1,2,0:T(8,128)S(1)} %copy.60) | copy-start | bytes 24580
  22.5 43.2 %copy-start.23 = (f32[1,8,2,128]{3,1,2,0:T(8,128)}, f32[1,8,2,128]{3,1,2,0:T(8,128)S(1)}, u32[]{:S(2)}) copy-start(f32[1,8,2,128]{3,1,2,0:T(8,128)S(1)} %copy.59) | copy-start | bytes 24580
  55.5 10.3 %copy-start.20 = (bf16[8,1,1664]{2,0,1:T(8,128)(2,1)}, bf16[8,1,1664]{2,0,1:T(8,128)(2,1)S(1)}, u32[]{:S(2)}) copy-start(bf16[8,1,1664]{2,0,1:T(8,128)(2,1)S(1)} %copy.58) | copy-start | bytes 79876
  55.5 7.6 copy-start.9
  55.6 10.2 %copy-start.27 = (f32[1024]{0:T(1024)}, f32[1024]{0:T(1024)S(1)}, u32[]{:S(2)}) copy-start(f32[1024]{0:T(1024)S(1)} %get-tuple-element.50) | copy-start | bytes 12292
  55.6 10.2 %copy-start.29 = (f32[1024]{0:T(1024)}, f32[1024]{0:T(1024)S(1)}, u32[]{:S(2)}) copy-start(f32[1024]{0:T(1024)S(1)} %get-tuple-element.53) | copy-start | bytes 12292
  63.1 3.7 copy-start.8
  162.4 19.9 %copy-start.6 = (f32[1024,128]{1,0:T(8,128)S(1)}, f32[1024,128]{1,0:T(8,128)}, u32[]{:S(2)}) copy-start(f32[1024,128]{1,0:T(8,128)} %get-tuple-element.63.cosines) | copy-start | bytes 1572868
  252.7 72.2 %copy-start.3 = (bf16[2,1024,512]{2,1,0:T(8,128)(2,1)}, bf16[2,1024,512]{2,1,0:T(8,128)(2,1)S(1)}, u32[]{:S(2)}) copy-start(bf16[2,1024,512]{2,1,0:T(8,128)(2,1)S(1)} %get-tuple-element.25) | copy-start | bytes 6291460
  323.6 1.3 copy-start.1
  324.9 1.4 copy-start.5
  412.8 2.2 copy-start
  510.2 14.7 %copy-start.10 = (f32[8,2,256,1024]{3,2,1,0:T(8,128)}, f32[8,2,256,1024]{3,2,1,0:T(8,128)S(1)}, u32[]{:S(2)}) copy-start(f32[8,2,256,1024]{3,2,1,0:T(8,128)S(1)} %fusion.68) | copy-start | bytes 50331652
  513.3 26.3 %collective-permute-start.4 = (bf16[8,256,1024]{2,1,0:T(8,128)(2,1)}, bf16[8,256,1024]{2,1,0:T(8,128)(2,1)}, u32[]{:S(2)}, u32[]{:S(2)}) collective-permute-start(bf16[8,256,1024]{2,1,0:T(8,128)(2,1)} %fusion.38), channel_id=1, source_target_pairs={{0,8},{8,0},{16,24},{24,16},{1,9},{9,1},{17,25},{25,17},{2,10},{10... | collective-permute-start | bytes 12582920 | tf_op jit(solution)/shard_map/ppermute | solution.py:171
  524.9 2.3 copy-start.13
  527.2 2.9 collective-permute-start.2
  533.0 232.4 %reduce-scatter.14.cloned.1.call-start = ((), (), s32[]{:S(2)}) async-start(), calls=%async_computation.13 | async-start | bytes 4718592 | tf_op jit(solution)/shard_map/reduce_scatter | solution.py:173
  547.9 244.6 %reduce-scatter.12.cloned.1.call-start = ((), (), s32[]{:S(2)}) async-start(), calls=%async_computation.12 | async-start | bytes 4718592 | tf_op jit(solution)/shard_map/reduce_scatter | solution.py:173
  569.5 5.7 copy-start.11
  577.9 7.4 collective-permute-start.3
  592.0 6.7 copy-start.33
  592.0 255.0 %reduce-scatter.8.cloned.1.call-start = ((), (), s32[]{:S(2)}) async-start(), calls=%async_computation.10 | async-start | bytes 1769472 | tf_op jit(solution)/shard_map/reduce_scatter | solution.py:173
  599.3 11.0 %copy-start.2 = (bf16[2,1024,512]{2,1,0:T(8,128)(2,1)S(1)}, bf16[2,1024,512]{2,1,0:T(8,128)(2,1)}, u32[]{:S(2)}) copy-start(bf16[2,1024,512]{2,1,0:T(8,128)(2,1)} %copy-done.1) | copy-start | bytes 6291460
  599.3 11.0 %copy-start.12 = (bf16[1024,2048]{1,0:T(8,128)(2,1)S(1)}, bf16[1024,2048]{1,0:T(8,128)(2,1)}, u32[]{:S(2)}) copy-start(bf16[1024,2048]{1,0:T(8,128)(2,1)} %copy.42) | copy-start | bytes 12582916
  599.3 11.0 %copy-start.16 = (bf16[2,1024,512]{2,1,0:T(8,128)(2,1)S(1)}, bf16[2,1024,512]{2,1,0:T(8,128)(2,1)}, u32[]{:S(2)}) copy-start(bf16[2,1024,512]{2,1,0:T(8,128)(2,1)} %get-tuple-element.31) | copy-start | bytes 6291460
  599.3 11.0 %copy-start.18 = (bf16[2,1024,512]{2,1,0:T(8,128)(2,1)S(1)}, bf16[2,1024,512]{2,1,0:T(8,128)(2,1)}, u32[]{:S(2)}) copy-start(bf16[2,1024,512]{2,1,0:T(8,128)(2,1)} %get-tuple-element.29) | copy-start | bytes 6291460
  609.4 9.9 %collective-permute-start.1 = (bf16[8,64,1536]{2,1,0:T(8,128)(2,1)S(1)}, bf16[8,64,1536]{2,1,0:T(8,128)(2,1)S(1)}, u32[]{:S(2)}, u32[]{:S(2)}) collective-permute-start(bf16[8,64,1536]{2,1,0:T(8,128)(2,1)S(1)} %fusion.45), channel_id=1, source_target_pairs={{0,8},{8,0},{16,24},{24,16},{1,9},{9,1},{17,25},{25,17},{2,10},{10... | collective-permute-start | bytes 4718600 | tf_op jit(solution)/shard_map/ppermute | solution.py:171
  620.8 293.9 %reduce-scatter.6.cloned.1.call-start = ((), (), s32[]{:S(2)}) async-start(), calls=%async_computation.9 | async-start | bytes 1769472 | tf_op jit(solution)/shard_map/reduce_scatter | solution.py:173
  621.3 8.8 copy-start.19
  624.7 6.9 copy-start.15
  624.7 28.6 %collective-permute-start = (bf16[8,64,1536]{2,1,0:T(8,128)(2,1)}, bf16[8,64,1536]{2,1,0:T(8,128)(2,1)}, u32[]{:S(2)}, u32[]{:S(2)}) collective-permute-start(bf16[8,64,1536]{2,1,0:T(8,128)(2,1)} %fusion.44), channel_id=1, source_target_pairs={{0,8},{8,0},{16,24},{24,16},{1,9},{9,1},{17,25},{25,17},{2,10},{10... | collective-permute-start | bytes 4718600 | tf_op jit(solution)/shard_map/ppermute | solution.py:171
  628.5 4.7 copy-start.17
  630.1 4.7 copy-start.14
  636.4 6.8 copy-start.4
  657.4 280.5 %all-gather.25.cloned.1.call-start = ((), (), s32[]{:S(2)}) async-start(), calls=%async_computation.15 | async-start | bytes 2621440 | tf_op jit(solution)/shard_map/all_gather | solution.py:174
  665.8 24.2 %copy-start.22 = (f32[1,8,2,128]{3,1,2,0:T(8,128)S(1)}, f32[1,8,2,128]{3,1,2,0:T(8,128)}, u32[]{:S(2)}) copy-start(f32[1,8,2,128]{3,1,2,0:T(8,128)} %copy-done.21) | copy-start | bytes 24580
  665.9 24.2 %copy-start.24 = (f32[1,8,2,128]{3,1,2,0:T(8,128)S(1)}, f32[1,8,2,128]{3,1,2,0:T(8,128)}, u32[]{:S(2)}) copy-start(f32[1,8,2,128]{3,1,2,0:T(8,128)} %copy-done.23) | copy-start | bytes 24580
  665.9 24.2 %copy-start.28 = (f32[1024]{0:T(1024)S(1)}, f32[1024]{0:T(1024)}, u32[]{:S(2)}) copy-start(f32[1024]{0:T(1024)} %copy-done.27) | copy-start | bytes 12292
  665.9 24.2 %copy-start.30 = (f32[1024]{0:T(1024)S(1)}, f32[1024]{0:T(1024)}, u32[]{:S(2)}) copy-start(f32[1024]{0:T(1024)} %copy-done.29) | copy-start | bytes 12292
  715.1 9.1 copy-start.31
  715.1 50.5 %copy-start.26 = (pred[2048]{0:T(1024)(128)(4,1)S(1)}, pred[2048]{0:T(1024)(128)(4,1)}, u32[]{:S(2)}) copy-start(pred[2048]{0:T(1024)(128)(4,1)} %copy-done.25) | copy-start | bytes 6148
  765.5 196.6 %all-gather.23.cloned.1.call-start = ((), (), s32[]{:S(2)}) async-start(), calls=%async_computation.14 | async-start | bytes 2621440 | tf_op jit(solution)/shard_map/all_gather | solution.py:174
  794.3 171.3 %copy-start.32 = (f32[128]{0:T(128)}, f32[128]{0:T(128)S(1)}, u32[]{:S(2)}) copy-start(f32[128]{0:T(128)S(1)} %get-tuple-element.89) | copy-start | bytes 1540
Sparse Core Ops, SparseCore 0:
  10.1 52.5 all-gather.16
  64.9 97.5 all-gather.14
  164.6 123.0 all-gather.18
  289.6 123.1 all-gather.20
  533.2 61.5 reduce-scatter.9
  598.7 87.0 reduce-scatter.13
  689.4 88.4 reduce-scatter.11
  782.3 64.5 reduce-scatter.7
  851.0 63.7 reduce-scatter.5
  916.3 21.5 all-gather.24
  939.5 22.5 all-gather.22

commit v2 on v1

--- a/solution.py
+++ b/solution.py
@@ -160,7 +160,7 @@
     )(mixed, mixed, mixed, grad_context, *tables)
 
 
-def reduce_owner(total):
+def chip_halves(total):
     copies, owners = lax.axis_size("rep"), lax.axis_size("fsdp")
     core = lax.axis_index("rep") % 2
     half = total.shape[0] // (2 * owners)
@@ -169,11 +169,38 @@
     theirs = lax.dynamic_index_in_dim(parts, 1 - core, 1, keepdims=False).astype(BF16)
     mine = lax.dynamic_index_in_dim(parts, core, 1, keepdims=False)
     got = lax.ppermute(theirs, "rep", [(i, i ^ 1) for i in range(copies)])
-    pair = (mine + got.astype(F32)).astype(BF16).reshape(owners * half, columns)
+    return (mine + got.astype(F32)).astype(BF16).reshape(owners * half, columns)
+
+
+def reduce_halves(pair):
+    copies, columns = lax.axis_size("rep"), pair.shape[1]
+    half = pair.shape[0] // lax.axis_size("fsdp")
     owned = lax.psum_scatter(pair, "fsdp", scatter_dimension=0, tiled=True)
     every = lax.all_gather(owned, "rep", axis=0, tiled=False).astype(F32)
     every = every.reshape(copies // 2, 2, half, columns)
     return jnp.sum(every, axis=0).reshape(2 * half, columns)
+
+
+def reduce_owner(total):
+    return reduce_halves(chip_halves(total))
+
+
+def gather_whole(shard, after=None):
+    if after is not None:
+        shard, _ = lax.optimization_barrier((shard, after))
+    copies, owners = lax.axis_size("rep"), lax.axis_size("fsdp")
+    core = lax.axis_index("rep") % 2
+    half, columns = shard.shape[0] // 2, shard.shape[1]
+    own = lax.dynamic_index_in_dim(shard.reshape(2, half, columns), core, 0, keepdims=False)
+    mine = lax.all_gather(own, "fsdp", axis=0, tiled=True)
+    got = lax.ppermute(mine, "rep", [(i, i ^ 1) for i in range(copies)])
+    mine_parts = mine.reshape(owners, half, columns)
+    got_parts = got.reshape(owners, half, columns)
+    first = core == 0
+    both = jnp.stack(
+        [jnp.where(first, mine_parts, got_parts), jnp.where(first, got_parts, mine_parts)], axis=1
+    )
+    return both.reshape(2 * owners * half, columns), mine
 
 
 def body(
@@ -204,10 +231,10 @@
         pieces.append(packed[:, at : at + size].reshape(owners * size))
         at += size
     gain_mlp, shift_mlp, up_bias, gain_attn, shift_attn, mix_bias, proj_bias, down_bias = pieces
-    up_full = lax.all_gather(up_weight, "fsdp", axis=0, tiled=True)
-    down_full = lax.all_gather(down_weight, "fsdp", axis=0, tiled=True)
-    proj_full = lax.all_gather(proj_weight, "fsdp", axis=0, tiled=True)
-    mix_full = lax.all_gather(mix_weight, "fsdp", axis=0, tiled=True)
+    up_full, done = gather_whole(up_weight)
+    down_full, done = gather_whole(down_weight)
+    mix_full, done = gather_whole(mix_weight, done)
+    proj_full, _ = gather_whole(proj_weight, done)
 
     places = jnp.arange(rows, dtype=jnp.int32)
     valid = (places[None, :] < lengths[:, None]).reshape(count, 1)
@@ -222,13 +249,15 @@
     second = (hat * g_mlp + shift_mlp.astype(F32)).astype(BF16)
 
     active, grad_hidden = mlp_front(second, outer, up_full, up_bias, down_full)
-    grad_down = reduce_owner(dot_tn(active, outer))
-    grad_up = reduce_owner(dot_tn(second, grad_hidden))
+    half_down = chip_halves(dot_tn(active, outer))
+    half_up = chip_halves(dot_tn(second, grad_hidden))
+    grad_down, grad_up = reduce_halves(half_down), reduce_halves(half_up)
     grad_second = dot_nt(grad_hidden, up_full)
     feed = dot_nn(active, down_full)
 
     mixed = (dot_nn(first, mix_full) + mix_bias.astype(F32)).reshape(batch, rows, 3 * width)
     grad_context = dot_nt(outer, proj_full).astype(BF16).reshape(batch, rows, width)
+    grad_context, _, _ = lax.optimization_barrier((grad_context, half_down, half_up))
     tables = rotary_tables(rows)
     share = width // GROUPS
     contexts, grads, mix_grads = [], [[], [], []], []

time: 978 us -> 910 us (0.930)
  waiting for transfers between devices: 302 us -> 195 us
  other arithmetic: 82.2 us -> 118 us
    all_gather x6, waiting for transfers between devices: 188 us -> 138 us  [the longest x4 110 us: gather_whole(): mine = lax.all_gather(own, 'fsdp', axis=0, tiled=True)]
    reduce_scatter x5, waiting for transfers between devices: 101 us -> 52.1 us  [reduce_halves(): owned = lax.psum_scatter(pair, 'fsdp', scatter_dimension=0, tiled=True)]
    another operation x0 -> x4, other arithmetic: none -> 15 us  [gather_whole(): jnp.stack([jnp.where(first, mine_parts, got_parts), jnp.where(first, got_...]
    select_n x0 -> x4, other arithmetic: none -> 14.3 us  [gather_whole(): jnp.where(first, mine_parts, got_parts)]
    convert_element_type x5 -> x6, other arithmetic: 23.5 us -> 28.9 us  [the longest x5 24.1 us: chip_halves(): return (mine + got.astype(F32)).astype(BF16).reshape(owners * half, columns)]
    unnamed x95 -> x111, local copies, waits for them, and re-layouts: 30.7 us -> 35.7 us
  transfers between devices with their start and end apart: 16 -> 20, of which waited for: 8 -> 7; matrix products, arithmetic and copies ran while one was open for 31% -> 42% of each run, Pallas kernels for 15% -> 21%
where the time goes in v2:
time: 910 us; the launch traced here: 903 us
  waiting for transfers between devices  195 us (21%)
  Pallas kernels  192 us (21%)
  matrix products  184 us (20%)
  other arithmetic  118 us (13%)
  local copies, waits for them, and re-layouts  99.5 us (11%)
  blocking collectives  95.6 us (11%)
  between operations  14.7 us (2%)
    pallas_call x2, Pallas kernels, attention(): pl.pallas_call(attention_kernel, grid=(batch, each), in_specs=[at(start),...  141 us
    all_gather x4, waiting for transfers between devices, gather_whole(): mine = lax.all_gather(own, 'fsdp', axis=0, tiled=True)  110 us
    dot_general x5, matrix products, dot_tn(): lax.dot_general(a, b, (((0,), (0,)), ((), ())), preferred_element_type=F32)  70.6 us
    dot_general x3, matrix products, dot_nt(): lax.dot_general(a, b, (((1,), (1,)), ((), ())), preferred_element_type=F32)  57 us
    dot_general x3, matrix products, dot_nn(): lax.dot_general(a, b, (((1,), (0,)), ((), ())), preferred_element_type=F32)  56.8 us
    reduce_scatter x5, waiting for transfers between devices, reduce_halves(): owned = lax.psum_scatter(pair, 'fsdp', scatter_dimension=0, tiled=True)  52.1 us
    pallas_call x1, Pallas kernels, mlp_front(): pl.pallas_call(mlp_kernel, grid=(wide // ft, rows // rt), in_specs=[pl.Bl...  51.3 us
    dot_general x4, local copies, waits for them, and re-layouts, dot_tn(): lax.dot_general(a, b, (((0,), (0,)), ((), ())), preferred_element_type=F32)  42.2 us
  transfers between devices with their start and end apart: 20, of which 7 were waited for; matrix products, arithmetic and copies ran while one was open for 42% of the time, Pallas kernels for 21%

profile of v2, /device:TPU:0, one launch (start us, length us, event | category | flops | bytes accessed | tf_op | source)
XLA Modules:
  0.0 903.2 jit_solution(15984638213071931745)
XLA Ops:
  9.3 1.9 constant_dynamic-slice_fusion
  11.3 75.6 %all-gather.19.cloned.1.call-done = bf16[1,2048,1024]{2,1,0:T(8,128)(2,1)} async-done(((bf16[1,256,1024]{2,1,0:T(8,128)(2,1)}), bf16[1,2048,1024]{2,1,0:T(8,128)(2,1)}) %all-gather.19.cloned.1.call-update) | async-done | bytes 4194320 | tf_op jit(solution)/shard_map/all_gather | solution.py:195
  93.6 30.9 %all-gather.10 = bf16[8,1,1664]{2,1,0:T(2,128)(2,1)S(1)} all-gather(bf16[1,1,1664]{2,1,0:T(2,128)(2,1)S(1)} %reshape.635), channel_id=2, replica_groups=mesh['rep'=4,'fsdp'=8] {'fsdp'}, dimensions={0}, use_global_device_ids=true | all-gather | bytes 29952 | tf_op jit(solution)/shard_map/all_gather | solution.py:228
  124.5 2.8 convert_reduce_fusion
  127.4 34.3 %all-gather.25.cloned.1.call-done = bf16[1,512,4096]{2,1,0:T(8,128)(2,1)} async-done(((bf16[1,64,4096]{2,1,0:T(8,128)(2,1)}), bf16[1,512,4096]{2,1,0:T(8,128)(2,1)}) %all-gather.25.cloned.1.call-update) | async-done | bytes 4194320 | tf_op jit(solution)/shard_map/all_gather | solution.py:195
  161.8 3.1 fusion.6
  165.3 3.0 fusion.18.second
  168.2 6.5 copy.43
  174.8 3.9 bitcast_select_fusion.outer
  179.7 5.1 broadcast_select_fusion.1
  184.7 6.5 pad_maximum_fusion.1
  191.2 5.8 broadcast_select_fusion.3
  197.0 7.8 pad_maximum_fusion
  204.8 51.3 %shard_map.254 = (bf16[2048,4096]{1,0:T(8,128)(2,1)}, bf16[2048,4096]{1,0:T(8,128)(2,1)}) custom-call(bf16[2048,1024]{1,0:T(8,128)(2,1)S(1)} %copy-done.2, bf16[2048,1024]{1,0:T(8,128)(2,1)} %bitcast_select_fusion.outer, bf16[1024,4096]{1,0:T(8,128)(2,1)} %bitcast.258, bf16[1,4096]{1,0:T(2,128)(2,1)S(1)} %bitcast.245, bf16[4096,1024]{1,0:T(8,128)(2,1)} %bitcast.256), custom_call_target="tpu_custom_call" | custom-call | flops 34359738368 | bytes 117440512 | tf_op jit(solution)/shard_map/pallas_call | solution.py:61
  256.2 21.5 %fusion = f32[8,2,64,4096]{3,2,1,0:T(8,128)S(1)} fusion(bf16[8,2,64,2048]{3,2,1,0:T(8,128)(2,1)} %bitcast.274, bf16[2048,4096]{1,0:T(8,128)(2,1)} %get-tuple-element.30), kind=kOutput, calls=%fused_computation | convolution fusion | flops 17179869184 | bytes 37748736 | tf_op jit(solution)/shard_map/dot_general | solution.py:32
  277.7 5.7 copy-done.11
  283.4 2.6 fusion.42
  286.7 4.8 fusion.69
  292.7 2.0 fusion.52
  294.7 4.8 fusion.9
  299.5 22.7 %copy.50 = bf16[4096,2048]{1,0:T(8,128)(2,1)} copy(bf16[4096,2048]{0,1:T(8,128)(2,1)} %bitcast.248) | data formatting | bytes 33554432 | tf_op jit(solution)/shard_map/dot_general | solution.py:32
  322.1 8.1 fusion.2
  330.3 21.5 %fusion.71 = f32[8,2,256,1024]{3,2,1,0:T(8,128)S(1)} fusion(bf16[8,2,256,2048]{3,2,1,0:T(8,128)(2,1)} %bitcast.249, bf16[2048,1024,1,1]{1,0,3,2:T(8,128)(2,1)} %bitcast.269), kind=kOutput, calls=%fused_computation.155 | convolution fusion | flops 17179869184 | bytes 37748736 | tf_op jit(solution)/shard_map/dot_general | solution.py:32
  351.8 5.8 copy-done.12
  357.6 2.6 fusion.41
  360.8 24.3 %fusion.72 = f32[2048,1024]{1,0:T(8,128)} fusion(bf16[2048,4096]{1,0:T(8,128)(2,1)} %get-tuple-element.30, bf16[1024,4096]{1,0:T(8,128)(2,1)} %bitcast.259), kind=kOutput, calls=%fused_computation.156 | convolution fusion | flops 17179869184 | bytes 33554432 | tf_op jit(solution)/shard_map/dot_general | solution.py:28
  385.5 9.0 %fusion.3 = bf16[8,256,1024]{2,1,0:T(8,128)(2,1)} fusion(bf16[8,256,1024]{2,1,0:T(8,128)(2,1)} %collective-permute-done.4, f32[8,2,256,1024]{3,2,1,0:T(8,128)} %copy-done.12, s32[]{:T(128)S(6)} %select_n.254), kind=kLoop, calls=%fused_computation.8 | loop fusion | flops 6291456 | bytes 16777220 | tf_op jit(solution)/shard_map/convert_element_type | solution.py:172
  394.6 6.2 convolution_convert_fusion
  400.9 3.3 broadcast_select_fusion.6
  404.7 19.7 %convolution_add_fusion = f32[2048,3072]{1,0:T(8,128)} fusion(bf16[2048,1024]{1,0:T(8,128)(2,1)} %bitcast.267, bf16[1024,3072]{1,0:T(8,128)(2,1)S(1)} %bitcast.261, f32[3072]{0:T(1024)S(1)} %reshape.597), kind=kOutput, calls=%fused_computation.2 | convolution fusion | flops 12891193344 | bytes 35663872 | tf_op jit(solution)/shard_map/dot_general | solution.py:24
  424.4 70.2 %shard_map.256 = (bf16[2,1024,512]{2,1,0:T(8,128)(2,1)S(1)}, bf16[2,1024,512]{2,1,0:T(8,128)(2,1)S(1)}, bf16[2,1024,512]{2,1,0:T(8,128)(2,1)}, bf16[2,1024,512]{2,1,0:T(8,128)(2,1)}) custom-call(f32[2,1024,3072]{2,1,0:T(8,128)} %bitcast.306, f32[2,1024,3072]{2,1,0:T(8,128)} %bitcast.307, f32[2,1024,3072]{2,1,0:T(8,128)} %bitcast.308, ...), custom_call_target="tpu_custom_call" | custom-call | flops 25769803776 | bytes 23068672 | tf_op jit(solution)/shard_map/pallas_call | solution.py:147
  496.9 70.9 %shard_map.255 = (bf16[2,1024,512]{2,1,0:T(8,128)(2,1)S(1)}, bf16[2,1024,512]{2,1,0:T(8,128)(2,1)S(1)}, bf16[2,1024,512]{2,1,0:T(8,128)(2,1)}, bf16[2,1024,512]{2,1,0:T(8,128)(2,1)}) custom-call(f32[2,1024,3072]{2,1,0:T(8,128)} %bitcast.309, f32[2,1024,3072]{2,1,0:T(8,128)} %bitcast.310, f32[2,1024,3072]{2,1,0:T(8,128)} %bitcast.311, ...), custom_call_target="tpu_custom_call" | custom-call | flops 25769803776 | bytes 23068672 | tf_op jit(solution)/shard_map/pallas_call | solution.py:147
  569.2 2.7 fusion.45
  571.9 6.6 copy.45
  578.5 7.5 fusion.73
  587.4 1.6 constant_dynamic-update-slice_fusion.5
  592.8 1.6 constant_dynamic-update-slice_fusion.2
  597.7 26.5 %fusion.66 = (bf16[1024]{0:T(1024)(128)(2,1)S(1)}, bf16[1024]{0:T(1024)(128)(2,1)S(1)}, f32[2048]{0:T(1024)S(1)}, f32[2048]{0:T(1024)S(1)}, f32[2048,1024]{1,0:T...) fusion(f32[2048]{0:T(1024)S(1)} %copy-done.27, ...), kind=kOutput, calls=%fused_computation.150 | convolution fusion | flops 12922642432 | bytes 44093440 | tf_op jit(solution)/shard_map/dot_general | solution.py:28
  624.3 6.5 copy.44
  630.8 10.4 %fusion.36 = f32[8,2,64,1536]{3,2,1,0:T(8,128)S(1)} fusion(bf16[8,2,64,2048]{3,2,1,0:T(8,128)(2,1)} %bitcast.272, bf16[2048,512]{1,0:T(8,128)(2,1)} %bitcast.293, bf16[2048,512]{1,0:T(8,128)(2,1)} %bitcast.291, bf16[2048,512]{1,0:T(8,128)(2,1)} %bitcast.239), kind=kOutput, calls=%fused_computation.51 | convolution fusion | flops 6461325312 | bytes 16777216 | tf_op jit(solution)/shard_map/dot_general | solution.py:32
  641.2 2.7 copy-done.15
  647.1 1.9 collective-permute-done.7
  649.0 4.0 fusion.43
  653.0 9.7 %fusion.31 = f32[8,2,64,1536]{3,2,1,0:T(8,128)S(1)} fusion(bf16[8,2,64,2048]{3,2,1,0:T(8,128)(2,1)} %bitcast.273, bf16[2048,512]{1,0:T(8,128)(2,1)} %bitcast.287, bf16[2048,512]{1,0:T(8,128)(2,1)} %bitcast.285, bf16[2048,512]{1,0:T(8,128)(2,1)S(1)} %bitcast.238), kind=kOutput, calls=%fused_computation.45 | convolution fusion | flops 6461325312 | bytes 16777216 | tf_op jit(solution)/shard_map/dot_general | solution.py:32
  663.3 3.1 collective-permute-done.6
  666.4 1.7 fusion.44
  669.5 8.9 reduce.3
  678.4 6.7 reduce.4
  685.2 34.3 %all-reduce = bf16[8,1536]{1,0:T(8,128)(2,1)S(1)} all-reduce(bf16[8,1536]{1,0:T(8,128)(2,1)S(1)} %constant_dynamic-update-slice_fusion.6), channel_id=14, replica_groups=mesh['rep'=4,'fsdp'=8] {'fsdp'}, use_global_device_ids=true, to_apply=%region_15.16.clone | all-reduce | flops 12288 | bytes 49152
  720.1 5.2 all-gather.11
  727.1 10.2 %fusion.46 = f32[2048,1024]{1,0:T(8,128)} fusion(bf16[1024,1024]{1,0:T(8,128)(2,1)} %bitcast.284, bf16[2048,512]{1,0:T(8,128)(2,1)S(1)} %bitcast.242, bf16[2048,512]{1,0:T(8,128)(2,1)} %bitcast.244), kind=kOutput, calls=%fused_computation.77 | convolution fusion | flops 4303355904 | bytes 14680064 | tf_op jit(solution)/shard_map/dot_general | solution.py:24
  737.6 27.0 %fusion.30 = bf16[2048,1024]{1,0:T(8,128)(2,1)} fusion(f32[2048,1024]{1,0:T(8,128)} %fusion.46, bf16[2,1024,1024]{2,1,0:T(8,128)(2,1)} %param.15, bf16[2048,4096]{1,0:T(8,128)(2,1)} %get-tuple-element.29, bf16[4096,1024]{1,0:T(8,128)(2,1)} %bitcast.257, f32[1024]{0:T(1024)S(1)} %add_bitcast_fusion, pred[2048]{0:T(1024)(128)(4,1)S(1)} %copy-done.32), kind=kOutput, calls=%fused_computation.39 | convolution fusion | flops 17192452096 | bytes 41949184 | tf_op jit(solution)/shard_map/dot_general | solution.py:24
  764.6 10.0 %fusion.22 = f32[2048,1024]{1,0:T(8,128)} fusion(bf16[2,1024,1024]{2,1,0:T(8,128)(2,1)} %param.15, f32[2048,1024]{1,0:T(8,128)} %get-tuple-element.51, f32[2048]{0:T(1024)S(1)} %broadcast_multiply_fusion, f32[2048]{0:T(1024)S(1)} %broadcast_multiply_fusion.1, f32[2048]{0:T(1024)S(1)} %copy-done.27, f32[2048]{0:T(1024)S(1)} %copy-done.29, ...), kind=kLoop, calls=%fused_computation.31 | loop fusion | flops 20971520 | bytes 25200640 | tf_op jit(solution)/shard_map/add | solution.py:287
  774.6 7.4 all-gather.7
  782.9 8.9 all-gather.6
  792.9 52.1 %reduce-scatter.6.cloned.1.call-done = bf16[64,1536]{1,0:T(8,128)(2,1)} async-done(((bf16[512,1536]{1,0:T(8,128)(2,1)}), bf16[64,1536]{1,0:T(8,128)(2,1)}) %reduce-scatter.6.cloned.1.call-update) | async-done | bytes 196624 | tf_op jit(solution)/shard_map/reduce_scatter | solution.py:178
  845.0 8.8 all-gather.5
  854.0 1.8 stack_reshape_reshape.6
  855.8 2.6 pad_maximum_fusion.6
  858.3 2.5 reshape.576
  860.8 7.2 all-gather.27.cloned.1.call-done
  868.1 3.6 convert_reduce_fusion.2
  871.6 20.7 %all-gather.29.cloned.1.call-done = bf16[1024,1024]{1,0:T(8,128)(2,1)} async-done(((bf16[256,1024]{1,0:T(8,128)(2,1)}), bf16[1024,1024]{1,0:T(8,128)(2,1)}) %all-gather.29.cloned.1.call-update) | async-done | bytes 2097168 | tf_op jit(solution)/shard_map/all_gather | solution.py:179
  892.3 3.6 convert_reduce_fusion.1
  (188 shorter events, 36.3 us)
Async XLA Ops:
  7.2 1.2 copy-start
  7.2 154.5 %copy-start.40 = (s32[2]{0:T(128)S(1)}, s32[2]{0:T(128)}, u32[]{:S(2)}) copy-start(s32[2]{0:T(128)} %param.16) | copy-start | bytes 28
  7.2 79.7 %all-gather.19.cloned.1.call-start = ((), (), s32[]{:S(2)}) async-start(), calls=%async_computation.10 | async-start | bytes 4718592 | tf_op jit(solution)/shard_map/all_gather | solution.py:195
  9.3 152.4 %all-gather.25.cloned.1.call-start = ((), (), s32[]{:S(2)}) async-start(), calls=%async_computation.13 | async-start | bytes 4718592 | tf_op jit(solution)/shard_map/all_gather | solution.py:195
  11.2 280.3 %all-gather.21.cloned.1.call-start = ((), (), s32[]{:S(2)}) async-start(), calls=%async_computation.11 | async-start | bytes 3538944 | tf_op jit(solution)/shard_map/all_gather | solution.py:195
  86.9 92.8 %collective-permute-start.3 = (bf16[2048,1024]{1,0:T(8,128)(2,1)}, bf16[2048,1024]{1,0:T(8,128)(2,1)}, u32[]{:S(2)}, u32[]{:S(2)}) collective-permute-start(bf16[2048,1024]{1,0:T(8,128)(2,1)} %bitcast.266), channel_id=1, source_target_pairs={{0,8},{8,0},{16,24},{24,16},{1,9},{9,1},{17,25},{25,17},{2,10},{10... | collective-permute-start | bytes 12582920 | tf_op jit(solution)/shard_map/ppermute | solution.py:196
  124.5 162.2 %copy-start.25 = (bf16[8,1,1664]{2,0,1:T(8,128)(2,1)}, bf16[8,1,1664]{2,0,1:T(8,128)(2,1)S(1)}, u32[]{:S(2)}) copy-start(bf16[8,1,1664]{2,0,1:T(8,128)(2,1)S(1)} %copy.58) | copy-start | bytes 79876
  161.7 29.5 %collective-permute-start.2 = (bf16[512,4096]{1,0:T(8,128)(2,1)}, bf16[512,4096]{1,0:T(8,128)(2,1)}, u32[]{:S(2)}, u32[]{:S(2)}) collective-permute-start(bf16[512,4096]{1,0:T(8,128)(2,1)} %bitcast.265), channel_id=1, source_target_pairs={{0,8},{8,0},{16,24},{24,16},{1,9},{9,1},{17,25},{25,17},{2,10},{10... | collective-permute-start | bytes 12582920 | tf_op jit(solution)/shard_map/ppermute | solution.py:196
  161.8 13.0 %copy-start.31 = (pred[2048]{0:T(1024)(128)(4,1)}, pred[2048]{0:T(1024)(128)(4,1)S(1)}, u32[]{:S(2)}) copy-start(pred[2048]{0:T(1024)(128)(4,1)S(1)} %lt.130) | copy-start | bytes 6148
  161.8 3.5 copy-start.10
  165.0 3.2 copy-start.33
  165.0 129.7 %copy-start.35 = (f32[1024]{0:T(1024)}, f32[1024]{0:T(1024)S(1)}, u32[]{:S(2)}) copy-start(f32[1024]{0:T(1024)S(1)} %get-tuple-element.65) | copy-start | bytes 12292
  165.0 129.7 %copy-start.37 = (f32[1024]{0:T(1024)}, f32[1024]{0:T(1024)S(1)}, u32[]{:S(2)}) copy-start(f32[1024]{0:T(1024)S(1)} %get-tuple-element.66) | copy-start | bytes 12292
  165.1 3.2 copy-start.26
  165.1 3.2 copy-start.28
  174.8 3.9 copy-start.24
  179.4 181.3 %all-gather.23.cloned.1.call-start = ((), (), s32[]{:S(2)}) async-start(), calls=%async_computation.12 | async-start | bytes 1179648 | tf_op jit(solution)/shard_map/all_gather | solution.py:195
  197.0 7.8 copy-start.2
  277.7 5.7 copy-start.11
  286.0 36.1 %collective-permute-start.5 = (bf16[8,64,4096]{2,1,0:T(8,128)(2,1)}, bf16[8,64,4096]{2,1,0:T(8,128)(2,1)}, u32[]{:S(2)}, u32[]{:S(2)}) collective-permute-start(bf16[8,64,4096]{2,1,0:T(8,128)(2,1)} %fusion.42), channel_id=1, source_target_pairs={{0,8},{8,0},{16,24},{24,16},{1,9},{9,1},{17,25},{25,17},{2,10},{10... | collective-permute-start | bytes 12582920 | tf_op jit(solution)/shard_map/ppermute | solution.py:171
  286.7 4.8 copy-start.30
  292.2 445.0 %reduce-scatter.12.cloned.1.call-start = ((), (), s32[]{:S(2)}) async-start(), calls=%async_computation.8 | async-start | bytes 4718592 | tf_op jit(solution)/shard_map/reduce_scatter | solution.py:178
  294.7 129.7 %copy-start.8 = (f32[1024,128]{1,0:T(8,128)}, f32[1024,128]{1,0:T(8,128)S(1)}, u32[]{:S(2)}) copy-start(f32[1024,128]{1,0:T(8,128)S(1)} %get-tuple-element.76.behind) | copy-start | bytes 1572868
  330.2 434.3 %reduce-scatter.14.cloned.1.call-start = ((), (), s32[]{:S(2)}) async-start(), calls=%async_computation.9 | async-start | bytes 4718592 | tf_op jit(solution)/shard_map/reduce_scatter | solution.py:178
  351.8 5.8 copy-start.12
  360.2 25.3 %collective-permute-start.4 = (bf16[8,256,1024]{2,1,0:T(8,128)(2,1)}, bf16[8,256,1024]{2,1,0:T(8,128)(2,1)}, u32[]{:S(2)}, u32[]{:S(2)}) collective-permute-start(bf16[8,256,1024]{2,1,0:T(8,128)(2,1)} %fusion.41), channel_id=1, source_target_pairs={{0,8},{8,0},{16,24},{24,16},{1,9},{9,1},{17,25},{25,17},{2,10},{10... | collective-permute-start | bytes 12582920 | tf_op jit(solution)/shard_map/ppermute | solution.py:171
  360.3 40.5 %collective-permute-start = (bf16[512,3072]{1,0:T(8,128)(2,1)}, bf16[512,3072]{1,0:T(8,128)(2,1)}, u32[]{:S(2)}, u32[]{:S(2)}) collective-permute-start(bf16[512,3072]{1,0:T(8,128)(2,1)} %bitcast.281), channel_id=1, source_target_pairs={{0,8},{8,0},{16,24},{24,16},{1,9},{9,1},{17,25},{25,17},{2,10},{10... | collective-permute-start | bytes 9437192 | tf_op jit(solution)/shard_map/ppermute | solution.py:196
  360.8 24.4 %copy-start.23 = (bf16[1,512,1024]{2,1,0:T(8,128)(2,1)S(1)}, bf16[1,512,1024]{2,1,0:T(8,128)(2,1)}, u32[]{:S(2)}) copy-start(bf16[1,512,1024]{2,1,0:T(8,128)(2,1)} %all-gather.23.cloned.1.call-done) | copy-start | bytes 3145732
  360.8 24.4 %collective-permute-start.1 = (bf16[512,1024]{1,0:T(8,128)(2,1)}, bf16[512,1024]{1,0:T(8,128)(2,1)S(1)}, u32[]{:S(2)}, u32[]{:S(2)}) collective-permute-start(bf16[512,1024]{1,0:T(8,128)(2,1)} %bitcast.297), channel_id=1, source_target_pairs={{0,8},{8,0},{16,24},{24,16},{1,9},{9,1},{17,25},{25,17},{2,10},{10... | collective-permute-start | bytes 3145736 | tf_op jit(solution)/shard_map/ppermute | solution.py:196
  385.5 9.1 %copy-start.18 = (bf16[8,2,64,1024]{3,2,1,0:T(8,128)(2,1)}, bf16[8,2,64,1024]{3,2,1,0:T(8,128)(2,1)S(1)}, u32[]{:S(2)}) copy-start(bf16[8,2,64,1024]{3,2,1,0:T(8,128)(2,1)S(1)} %pad_maximum_fusion.5) | copy-start | bytes 6291460
  385.5 9.1 %copy-start.14 = (bf16[2,1024,1024]{2,1,0:T(8,128)(2,1)S(1)}, bf16[2,1024,1024]{2,1,0:T(8,128)(2,1)}, u32[]{:S(2)}) copy-start(bf16[2,1024,1024]{2,1,0:T(8,128)(2,1)} %get-tuple-element.47) | copy-start | bytes 12582916
  400.8 373.8 %reduce-scatter.10.cloned.1.call-start = ((), (), s32[]{:S(2)}) async-start(), calls=%async_computation.7 | async-start | bytes 1179648 | tf_op jit(solution)/shard_map/reduce_scatter | solution.py:178
  404.7 19.7 %copy-start.13 = (bf16[8,2,64,3072]{3,2,1,0:T(8,128)(2,1)}, bf16[8,2,64,3072]{3,2,1,0:T(8,128)(2,1)S(1)}, u32[]{:S(2)}) copy-start(bf16[8,2,64,3072]{3,2,1,0:T(8,128)(2,1)S(1)} %pad_maximum_fusion.2) | copy-start | bytes 18874372
  494.6 1.3 copy-start.3
  495.9 1.0 copy-start.9
  496.9 71.0 %copy-start.5 = (bf16[2,1024,512]{2,1,0:T(8,128)(2,1)}, bf16[2,1024,512]{2,1,0:T(8,128)(2,1)S(1)}, u32[]{:S(2)}) copy-start(bf16[2,1024,512]{2,1,0:T(8,128)(2,1)S(1)} %get-tuple-element.33) | copy-start | bytes 6291460
  567.9 1.4 copy-start.7
  586.0 4.7 copy-start.16
  586.0 3.1 copy-start.4
  587.2 58.3 %collective-permute-start.8 = (bf16[8,64,1024]{2,1,0:T(8,128)(2,1)}, bf16[8,64,1024]{2,1,0:T(8,128)(2,1)S(1)}, u32[]{:S(2)}, u32[]{:S(2)}) collective-permute-start(bf16[8,64,1024]{2,1,0:T(8,128)(2,1)} %fusion.50), channel_id=1, source_target_pairs={{0,8},{8,0},{16,24},{24,16},{1,9},{9,1},{17,25},{25,17},{2,10},{10... | collective-permute-start | bytes 3145736 | tf_op jit(solution)/shard_map/ppermute | solution.py:171
  587.4 3.8 copy-start.19
  589.1 3.7 copy-start.21
  591.3 3.2 copy-start.20
  592.8 3.2 copy-start.22
  594.5 3.2 copy-start.27
  594.5 3.2 copy-start.29
  594.5 3.2 copy-start.34
  594.5 3.2 copy-start.36
  594.5 3.2 copy-start.38
  630.8 14.7 %copy-start.17 = (f32[8,2,64,1024]{3,2,1,0:T(8,128)S(1)}, f32[8,2,64,1024]{3,2,1,0:T(8,128)}, u32[]{:S(2)}) copy-start(f32[8,2,64,1024]{3,2,1,0:T(8,128)} %copy-done.16) | copy-start | bytes 12582916
  641.2 2.7 copy-start.15
  645.2 3.8 collective-permute-start.7
  646.9 136.0 %reduce-scatter.8.cloned.1.call-start = ((), (), s32[]{:S(2)}) async-start(), calls=%async_computation.6 | async-start | bytes 1769472 | tf_op jit(solution)/shard_map/reduce_scatter | solution.py:178
  652.9 192.1 %reduce-scatter.6.cloned.1.call-start = ((), (), s32[]{:S(2)}) async-start(), calls=%async_computation.5 | async-start | bytes 1769472 | tf_op jit(solution)/shard_map/reduce_scatter | solution.py:178
  662.9 5.3 copy-start.42
  662.9 3.5 collective-permute-start.6
  668.1 199.9 %all-gather.27.cloned.1.call-start = ((), (), s32[]{:S(2)}) async-start(), calls=%async_computation.14 | async-start | bytes 2621440 | tf_op jit(solution)/shard_map/all_gather | solution.py:179
  678.3 6.8 copy-start.39
  678.4 48.7 %copy-start.6 = (bf16[2,1024,512]{2,1,0:T(8,128)(2,1)S(1)}, bf16[2,1024,512]{2,1,0:T(8,128)(2,1)}, u32[]{:S(2)}) copy-start(bf16[2,1024,512]{2,1,0:T(8,128)(2,1)} %copy-done.5) | copy-start | bytes 6291460
  727.1 168.8 %copy-start.41 = (f32[128]{0:T(128)}, f32[128]{0:T(128)S(1)}, u32[]{:S(2)}) copy-start(f32[128]{0:T(128)S(1)} %get-tuple-element.106) | copy-start | bytes 1540
  727.1 10.5 %copy-start.32 = (pred[2048]{0:T(1024)(128)(4,1)S(1)}, pred[2048]{0:T(1024)(128)(4,1)}, u32[]{:S(2)}) copy-start(pred[2048]{0:T(1024)(128)(4,1)} %copy-done.31) | copy-start | bytes 6148
  737.3 155.0 %all-gather.29.cloned.1.call-start = ((), (), s32[]{:S(2)}) async-start(), calls=%async_computation.15 | async-start | bytes 2621440 | tf_op jit(solution)/shard_map/all_gather | solution.py:179
  868.1 28.3 %copy-start.1 = (bf16[512,1024]{1,0:T(8,128)(2,1)S(1)}, bf16[512,1024]{1,0:T(8,128)(2,1)}, u32[]{:S(2)}) copy-start(bf16[512,1024]{1,0:T(8,128)(2,1)} %param.24) | copy-start | bytes 3145732
Sparse Core Ops, SparseCore 0:
  10.7 76.0 all-gather.18
  89.6 72.0 all-gather.24
  179.5 58.8 all-gather.20
  292.4 38.4 all-gather.22
  334.3 86.7 reduce-scatter.11
  425.1 87.8 reduce-scatter.13
  647.0 61.8 reduce-scatter.9
  713.3 63.9 reduce-scatter.7
  781.3 63.6 reduce-scatter.5
  846.5 21.5 all-gather.26
  869.7 22.5 all-gather.28
